TPU v7x, 256 devices: a whole 4x4x8 slice. The times are simulated.
256 devices in a mesh: sample: 32 (over x_lo, z, core), block: 8 (over x_hi, y).
Axes of the slice: x: 4 (x_hi: 2, x_lo: 2; x = x_hi * 2 + x_lo), y: 4, z: 8, core: 2. Of those that a mesh axis runs over, the one named last changes fastest.
Arguments:
- genotype: int32 [32768, 8000], P('sample', 'block'), may hold values from 0 to 2
- allele_freq: float32 [8000], P('block'), may hold values from 0.05 to 0.5
- phenotype: bfloat16 [32768, 16], P('sample'), may hold values from -6 to 6
- shrinkage: float32 [2], replicated, may hold values from 0.05 to 2
- owner_order: int32 [16], replicated, may hold values from 0 to 15, each once
Outputs:
- predictions: bfloat16 [16, 32, 32768], P('block', None, 'sample')
Inputs may be any that keep to these rules, and one draw needn't show every extreme that they name: `owner_order`: each phenotype appears once.
All inputs are finite; a program needn't handle non-finite values.
Results may differ from a plain program's by a relative error of at most 0.0056.
Values may be sent and summed in bfloat16 or wider, within the bound.
A program may use at most 128 MiB of HBM per device.

v0:
```python
import jax
import jax.numpy as jnp
from jax import lax
from jax.sharding import PartitionSpec as P

SNPS = 500
FOLDS = 5


def standardize(genotype, allele_freq):
    spread = jnp.sqrt(2.0 * allele_freq * (1.0 - allele_freq))
    return ((genotype.astype(jnp.float32) - 2.0 * allele_freq) / spread).astype(jnp.bfloat16)


def solve_pair(factor, target):
    return jax.scipy.linalg.cho_solve((factor, True), target)


def predict(columns, weights):
    stacked = jnp.transpose(weights, (2, 0, 1)).reshape(-1, weights.shape[1])
    product = lax.dot_general(
        stacked, columns, (((1,), (1,)), ((), ())), preferred_element_type=jnp.float32
    )
    return product.astype(jnp.bfloat16).reshape(
        weights.shape[2], weights.shape[0], columns.shape[0]
    )


def inner_products(left_cols, right_cols):
    return lax.dot_general(
        left_cols, right_cols, (((0,), (0,)), ((), ())), preferred_element_type=jnp.float32
    )


def tile_pairs():
    pairs = []
    for row_tile in range(4):
        for col_tile in range(row_tile, 4):
            pairs.append((row_tile, col_tile))
    return pairs


def tile_grams(left_cols, right_cols, tile_width):
    tile_list = []
    for row_tile, col_tile in tile_pairs():
        first = left_cols[:, row_tile * tile_width : (row_tile + 1) * tile_width]
        second = right_cols[:, col_tile * tile_width : (col_tile + 1) * tile_width]
        tile_list.append(inner_products(first, second))
    return jnp.stack(tile_list)


def rebuild(tile_stack):
    pairs = tile_pairs()
    band_rows = []
    for row_tile in range(4):
        band_row = []
        for col_tile in range(4):
            if row_tile <= col_tile:
                band_row.append(tile_stack[pairs.index((row_tile, col_tile))])
            else:
                band_row.append(jnp.transpose(tile_stack[pairs.index((col_tile, row_tile))]))
        band_rows.append(jnp.concatenate(band_row, axis=1))
    return jnp.concatenate(band_rows, axis=0)


def shared_solve(rest_grams, rest_crosses, shrinkage, counts):
    member_count = rest_grams.shape[1]
    width = rest_grams.shape[-1]
    traits = rest_crosses.shape[-1]
    ridge_count = shrinkage.shape[0]
    systems = FOLDS * member_count * ridge_count
    devices = lax.axis_size("sample")
    share = -(-systems // devices)
    flat_grams = rest_grams.reshape(FOLDS * member_count, width, width)
    flat_crosses = rest_crosses.reshape(FOLDS * member_count, width, traits)
    flat_counts = jnp.repeat(counts, member_count)
    owned_ids = lax.axis_index("sample") * share + lax.broadcasted_iota(jnp.int32, (share,), 0)
    owned_ids = jnp.minimum(owned_ids, systems - 1)
    pair_ids = owned_ids // ridge_count
    ridge_ids = owned_ids % ridge_count
    chosen_counts = jnp.take(flat_counts, pair_ids, axis=0)
    system = jnp.take(flat_grams, pair_ids, axis=0) / chosen_counts[:, None, None]
    target = jnp.take(flat_crosses, pair_ids, axis=0) / chosen_counts[:, None, None]
    identity = jnp.eye(width, dtype=jnp.float32)
    full = system + jnp.take(shrinkage, ridge_ids, axis=0)[:, None, None] * identity
    factor = jnp.linalg.cholesky(full)
    solved = jax.vmap(solve_pair, (0, 0))(factor, target).astype(jnp.bfloat16)
    collected = lax.all_gather(solved, "sample", axis=0, tiled=True)
    return collected[:systems].reshape(FOLDS, member_count, ridge_count, width, traits)


def shards(genotype, allele_freq, phenotype, shrinkage, owner_order):
    sample_rows = genotype.shape[0]
    total_rows = sample_rows * lax.axis_size("sample")
    scaled = standardize(genotype, allele_freq)
    ordered = jnp.take(phenotype, owner_order, axis=1)
    local_blocks = allele_freq.shape[0] // SNPS
    tile_width = SNPS // 4
    column_sets = [scaled[:, member * SNPS : (member + 1) * SNPS] for member in range(local_blocks)]
    bounds = [-(-(k * total_rows) // FOLDS) for k in range(FOLDS + 1)]
    counts = jnp.array(
        [float(total_rows - (bounds[k + 1] - bounds[k])) for k in range(FOLDS)], dtype=jnp.float32
    )
    start_row = lax.axis_index("sample") * sample_rows
    row_ids = start_row + lax.broadcasted_iota(jnp.int32, (sample_rows,), 0)
    fold_of = row_ids * FOLDS // total_rows
    first_fold = start_row * FOLDS // total_rows
    slot_folds = [first_fold, first_fold + 1]
    slot_masks = [fold_of == slot_folds[0], fold_of == slot_folds[1]]
    picked = jnp.minimum(jnp.stack(slot_folds), FOLDS - 1)
    fold_ids = jnp.arange(FOLDS, dtype=jnp.int32)

    def fold_partials(member):
        columns = column_sets[member]
        gram_total = jnp.zeros((FOLDS, 10, tile_width, tile_width), jnp.float32)
        cross_total = jnp.zeros((FOLDS, SNPS, ordered.shape[1]), jnp.float32)
        for slot in range(2):
            masked = jnp.where(slot_masks[slot][:, None], columns, jnp.zeros_like(columns))
            selector = (fold_ids == slot_folds[slot]).astype(jnp.float32)
            gram_total = (
                gram_total
                + selector[:, None, None, None] * tile_grams(masked, columns, tile_width)[None]
            )
            cross_total = (
                cross_total + selector[:, None, None] * inner_products(masked, ordered)[None]
            )
        return (gram_total, cross_total)

    def weights_for(members):
        parts = [fold_partials(member) for member in members]
        grams = jnp.stack([item[0] for item in parts], axis=1)
        crosses = jnp.stack([item[1] for item in parts], axis=1)
        summed_grams, summed_crosses = lax.psum((grams, crosses), "sample")
        whole = jax.vmap(jax.vmap(rebuild))(summed_grams)
        rest_grams = jnp.sum(whole, axis=0)[None] - whole
        rest_crosses = jnp.sum(summed_crosses, axis=0)[None] - summed_crosses
        every_weights = shared_solve(rest_grams, rest_crosses, shrinkage, counts)
        return jnp.take(every_weights, picked, axis=0)

    def fold_predictions(member, slot_weights):
        columns = column_sets[member]
        lower = predict(columns, slot_weights[0])
        upper = predict(columns, slot_weights[1])
        return jnp.where(slot_masks[1][None, None, :], upper, lower)

    weights = weights_for(list(range(local_blocks)))
    local_preds = jnp.concatenate(
        [fold_predictions(member, weights[:, member]) for member in range(local_blocks)], axis=1
    )
    return lax.all_to_all(local_preds, "block", split_axis=0, concat_axis=1, tiled=True)


def solution(mesh):
    in_specs = (P("sample", "block"), P("block"), P("sample", None), P(), P())
    out_specs = P("block", None, "sample")
    return jax.shard_map(shards, mesh=mesh, in_specs=in_specs, out_specs=out_specs, check_vma=False)
```

profile of v0, /device:TPU:34, one launch (start us, length us, event | category | flops | bytes accessed | tf_op | source)
XLA Modules:
  0.0 543.6 jit_solution(14251529554659590960)
XLA Ops:
  8.6 2.7 divide_convert_fusion
  11.3 1.7 broadcast_select_fusion.3
  15.5 1.7 fusion.186
  17.3 1.6 fusion.184
  30.7 1.0 multiply_add_fusion.1
  31.7 3.5 pad_maximum_fusion
  38.7 238.9 %all-reduce.6.cloned.1.call-done = (f32[5,2,10,125,125]{4,3,1,0,2:T(8,128)}, f32[5,2,500,16]{2,3,1,0:T(8,128)}) async-done(((f32[5,2,10,125,125]{4,3,1,0,2:T(8,128)}, f32[5,2,500,16]{2,3,1,0:T(8,128)}), (f32[5,2,10,125,125]{4,3,1,0,2:T(8,128)}, f32[5,2,500,16]{2,3,1,0:T(8,128)})) %all-reduce.6.cloned.1.call-update) | async-done | bytes 6570016 | tf_op jit(solution)/shard_map/psum | solution.py:133
  277.7 7.3 %slice_bitcast_fusion.46 = (f32[5,2,125,125]{3,2,1,0:T(8,128)}, f32[5,2,125,125]{3,2,1,0:T(8,128)}, f32[5,2,125,125]{2,3,1,0:T(8,128)}, f32[5,2,125,125]{3,2,1,0...) fusion(f32[5,2,10,125,125]{4,3,1,0,2:T(8,128)} %get-tuple-eleme, ...), kind=kLoop, calls=%fused_computation.367 | loop fusion | bytes 18125000 | tf_op jit(solution)/shard_map/vmap(vmap())/squeeze | solution.py:59
  285.9 1.4 copy.84
  287.2 2.2 copy.86
  289.4 2.2 copy.66
  291.6 2.2 copy.67
  293.9 2.4 copy.68
  296.2 2.3 copy.83
  298.5 3.0 pad_maximum_fusion.1
  301.6 3.3 copy.69
  304.9 13.1 %maximum_reduce_fusion = f32[2,500,500]{2,1,0:T(8,128)S(1)} fusion(f32[5,2,125,125]{3,2,1,0:T(8,128)} %get-tuple-element.77, f32[5,2,125,125]{3,2,1,0:T(8,128)} %copy.68, f32[5,2,125,125]{3,2,1,0:T(8,128)} %copy.67, f32[5,2,125,125]{3,2,1,0:T(8,128)} %bitcast.442, f32[5,2,125,125]{3,2,1,0:T(8,128)} %get-tuple-element.74, ...), kind=kLoop, calls=%fused_computation.4 | loop fusion | flops 32000000 | bytes 12000000 | tf_op jit(solution)/shard_map/reduce_sum | solution.py:135
  318.1 1.3 sub.54
  321.6 1.5 select_add_fusion
  323.2 2.6 copy.77
  325.8 1.5 fusion.68
  327.3 1.0 copy-done.17
  328.3 11.7 %custom-call.38 = f32[1,128,128]{2,1,0:T(8,128)S(1)} custom-call(f32[1,128,128]{2,1,0:T(8,128)S(1)} %cholesky.267), custom_call_target="Cholesky" | custom-call | tf_op jit(solution)/shard_map/jit(cholesky)/cholesky | solution.py:86
  344.4 10.6 %custom-call.39 = f32[1,1,128,128]{2,3,1,0:T(8,128)S(1)} custom-call(f32[1,1,128,128]{3,2,1,0:T(8,128)} %get-tuple-element.105), custom_call_target="InvertDiagBlocksLowerTriangular" | custom-call | tf_op jit(solution)/shard_map/jit(cholesky)/cholesky | solution.py:86
  355.1 1.4 constant_dynamic-update-slice_fusion.3
  356.5 1.4 fusion
  357.9 11.9 %custom-call.40 = f32[1,128,128]{2,1,0:T(8,128)S(1)} custom-call(f32[1,128,128]{2,1,0:T(8,128)S(1)} %cholesky.271), custom_call_target="Cholesky" | custom-call | tf_op jit(solution)/shard_map/jit(cholesky)/cholesky | solution.py:86
  370.5 9.8 %custom-call.41 = f32[1,1,128,128]{2,3,1,0:T(8,128)S(1)} custom-call(f32[1,1,128,128]{3,2,1,0:T(8,128)S(1)} %get-tuple-element.102), custom_call_target="InvertDiagBlocksLowerTriangular" | custom-call | tf_op jit(solution)/shard_map/jit(cholesky)/cholesky | solution.py:86
  380.7 1.3 fusion.2
  382.6 13.2 %custom-call.42 = f32[1,128,128]{2,1,0:T(8,128)} custom-call(f32[1,128,128]{2,1,0:T(8,128)} %cholesky.276), custom_call_target="Cholesky" | custom-call | tf_op jit(solution)/shard_map/jit(cholesky)/cholesky | solution.py:86
  395.8 1.5 select_reduce_fusion
  398.0 11.3 %custom-call.43 = f32[1,1,128,128]{2,3,1,0:T(8,128)} custom-call(f32[1,1,128,128]{3,2,1,0:T(8,128)} %get-tuple-element.99), custom_call_target="InvertDiagBlocksLowerTriangular" | custom-call | tf_op jit(solution)/shard_map/jit(cholesky)/cholesky | solution.py:86
  409.3 1.1 fusion.43
  410.4 1.2 fusion.44
  411.5 10.9 %custom-call.44 = f32[1,116,116]{2,1,0:T(8,128)S(1)} custom-call(f32[1,116,116]{2,1,0:T(8,128)S(1)} %fusion.44), custom_call_target="Cholesky" | custom-call | tf_op jit(solution)/shard_map/jit(cholesky)/cholesky | solution.py:86
  426.7 8.7 %while.5 = (s32[]{:T(128)}, f32[1,500,500]{2,1,0:T(8,128)}, s32[3,2]{0,1:T(2,128)S(1)}, f32[3,1,128,128]{3,2,1,0:T(8,128)S(1)}, s32[]{:T(128)}) while((s32[]{:T(128)}, f32[1,500,500]{2,1,0:T(8,128)}, s32[3,2]{0,1:T(2,128)S(1)}, f32[3,1,128,128]{3,2,1,0:T(8,128)S(1)}, s32[]{:T(128)}) %tuple.87), condition=%wide.while_cond.3, body=%wide.while_body.3.sunk | while | flops 2 | bytes 131189 | solution.py:16
  427.3 2.3 bitcast_dynamic-update-slice_fusion.2
  430.2 2.3 bitcast_dynamic-update-slice_fusion.2
  433.1 2.3 bitcast_dynamic-update-slice_fusion.2
  435.5 39.3 %custom-call.45 = f32[1,4,128,128]{2,3,1,0:T(8,128)S(1)} custom-call(f32[1,4,128,128]{3,2,1,0:T(8,128)S(1)} %pad_maximum_fusion.3), custom_call_target="InvertDiagBlocksLowerTriangular" | custom-call | tf_op jit(solution)/shard_map/vmap(jit(_cho_solve))/triangular_solve | solution.py:16
  475.0 1.0 fusion.50
  476.3 1.1 fusion.48
  477.6 1.2 fusion.46
  479.2 1.0 convolution_subtract_fusion.2
  480.4 1.1 convolution_subtract_fusion.1
  481.7 1.2 convolution_subtract_fusion
  483.2 35.6 %all_gather.3 = bf16[32,500,16]{1,2,0:T(8,128)(2,1)S(1)} all-gather(bf16[1,500,16]{1,2,0:T(8,128)(2,1)S(1)} %pad_maximum_fusion.5), channel_id=1, replica_groups=mesh['sample'=32,'block'=8] {'sample'}, dimensions={0}, use_global_device_ids=true | all-gather | bytes 528000 | tf_op jit(solution)/shard_map/all_gather | solution.py:88
  521.7 13.9 %all_to_all.18 = bf16[16,4,1024]{2,1,0:T(4,128)(2,1)S(1)} all-to-all(bf16[16,4,1024]{2,1,0:T(4,128)(2,1)S(1)} %pad_maximum_fusion.4), channel_id=1, replica_groups=mesh['sample'=32,'block'=8] {'block'}, dimensions={0} | all-to-all | bytes 262144 | tf_op jit(solution)/shard_map/all_to_all | solution.py:150
  (183 shorter events, 36.7 us)
Async XLA Ops:
  6.5 8.4 %copy-start = (bf16[1024,16]{0,1:T(8,128)(2,1)S(1)}, bf16[1024,16]{0,1:T(8,128)(2,1)}, u32[]{:S(2)}) copy-start(bf16[1024,16]{0,1:T(8,128)(2,1)} %param.8) | copy-start | bytes 98308
  6.5 271.1 %all-reduce.6.cloned.1.call-start = ((), (), s32[]{:S(2)}) async-start(), calls=%async_computation.1 | async-start | bytes 13762560 | tf_op jit(solution)/shard_map/psum | solution.py:133
  13.0 1.0 copy-start.15
  15.5 3.4 copy-start.14
  15.5 3.7 copy-start.13
  19.1 1.3 copy-start.16
  19.2 1.4 copy-start.25
  35.2 0.7 copy-start.28
  35.2 0.8 copy-start.29
  285.0 0.8 copy-start.4
  318.0 1.5 copy-start.2
  318.0 1.5 copy-start.5
  318.0 1.5 copy-start.6
  318.0 1.7 copy-start.7
  318.0 1.8 copy-start.8
  318.1 2.0 copy-start.9
  318.1 2.2 copy-start.10
  318.1 2.4 copy-start.11
  318.1 2.6 copy-start.18
  318.1 2.8 copy-start.19
  318.1 3.0 copy-start.20
  318.1 3.1 copy-start.21
  318.1 3.3 copy-start.22
  318.1 3.5 copy-start.23
  323.2 2.6 copy-start.3
  325.8 16.4 %copy-start.24 = (f32[5,2,500,16]{2,3,1,0:T(8,128)S(1)}, f32[5,2,500,16]{2,3,1,0:T(8,128)}, u32[]{:S(2)}) copy-start(f32[5,2,500,16]{2,3,1,0:T(8,128)} %get-tuple-element.66) | copy-start | bytes 960004
  327.3 1.0 copy-start.17
  340.0 0.6 copy-start.26
  380.6 46.0 %copy-start.27 = (f32[3,1,128,128]{3,2,1,0:T(8,128)S(1)}, f32[3,1,128,128]{3,2,1,0:T(8,128)}, u32[]{:S(2)}) copy-start(f32[3,1,128,128]{3,2,1,0:T(8,128)} %custom-call.54) | copy-start | bytes 589828
  425.7 1.0 copy-start.12
  520.5 15.8 %copy-start.1 = (bf16[1024,16]{0,1:T(8,128)(2,1)S(1)}, bf16[1024,16]{0,1:T(8,128)(2,1)}, u32[]{:S(2)}) copy-start(bf16[1024,16]{0,1:T(8,128)(2,1)} %param.8) | copy-start | bytes 98308
Sparse Core Ops, SparseCore 0:
  35.3 242.3 all-reduce.5
where the time goes:
time: 555 us; the launch traced here: 544 us
  waiting for transfers between devices  239 us (43%)
  other arithmetic  157 us (28%)
  blocking collectives  49.5 us (9%)
  local copies, waits for them, and re-layouts  48.5 us (9%)
  matrix products  31.1 us (6%)
  between operations  18.6 us (3%)
    psum x1, waiting for transfers between devices, weights_for(): summed_grams, summed_crosses = lax.psum((grams, crosses), 'sample')  239 us
    another operation x15, other arithmetic, shared_solve(): factor = jnp.linalg.cholesky(full)  84.2 us
    another operation x8, other arithmetic, solve_pair(): return jax.scipy.linalg.cho_solve((factor, True), target)  39.6 us
    all_gather x1, blocking collectives, shared_solve(): collected = lax.all_gather(solved, 'sample', axis=0, tiled=True)  35.6 us
    dot_general x44, matrix products, inner_products(): lax.dot_general(left_cols, right_cols, (((0,), (0,)), ((), ())), preferre...  14.8 us
    all_to_all x1, blocking collectives, shards(): lax.all_to_all(local_preds, 'block', split_axis=0, concat_axis=1, tiled=T...  13.9 us
    reduce_sum x1, other arithmetic, weights_for(): rest_grams = jnp.sum(whole, axis=0)[None] - whole  13.1 us
    unnamed x64, local copies, waits for them, and re-layouts  13 us
  transfers between devices with their start and end apart: 1, of which 1 were waited for; matrix products, arithmetic and copies ran while one was open for 0% of the time, Pallas kernels for 0%

commit v1 on v0

v1 whole, which is shorter than its diff:
```python
import functools

import jax
import jax.numpy as jnp
from jax import lax
from jax.experimental import pallas as pl
from jax.experimental.pallas import tpu as pltpu
from jax.sharding import PartitionSpec as P

SNPS = 500
FOLDS = 5
WIDE = 512
ROWS = 1024
CHIPS = 16
SLICE = 80
OUT_LANES = 512
MESH = pl.DeviceIdType.MESH
BF16 = jnp.bfloat16
I16 = jnp.int16

W = 128
TRAITS = 16
PAIRS = [(i, j) for i in range(4) for j in range(i, 4)]
F32 = jnp.float32
HI = lax.Precision.HIGHEST


def row_of(x, i):
    return jnp.broadcast_to(x[i : i + 1, :], x.shape)


def lane_of(x, k):
    return jnp.broadcast_to(x[:, k : k + 1], x.shape)


def invert(tiles):
    sub = lax.broadcasted_iota(jnp.int32, (8, W), 0)
    lane = lax.broadcasted_iota(jnp.int32, (8, W), 1)
    for j in range(16):
        inside = (lane >= 8 * j) & (lane < 8 * j + 8)
        panel = tiles[j]
        cols = [lane_of(panel, 8 * j + i) for i in range(8)]
        rows = jnp.where(inside, (lane - 8 * j == sub).astype(F32), panel)
        for i in range(8):
            here = sub == i
            recip = 1.0 / row_of(cols[i], i)
            q = row_of(rows, i) * recip
            rows = jnp.where(here, q, rows - cols[i] * q)
            for c in range(i + 1, 8):
                qc = row_of(cols[c], i) * recip
                cols[c] = jnp.where(here, qc, cols[c] - cols[i] * qc)
        spread = [row_of(rows, i) for i in range(8)]
        new = []
        for t in range(16):
            if t == j:
                new.append(rows)
                continue
            acc = lane_of(tiles[t], 8 * j) * spread[0]
            for i in range(1, 8):
                acc = acc + lane_of(tiles[t], 8 * j + i) * spread[i]
            new.append(jnp.where(inside, 0.0, tiles[t]) - acc)
        tiles = new
    return tiles


def solve_kernel(par_ref, gram_ref, cross_ref, vec_ref, out_ref, m_ref, c_ref, t_ref, d_ref):
    lam = par_ref[0]
    inv_n = 1.0 / par_ref[1]
    count = par_ref[1]
    eye = lax.broadcasted_iota(jnp.int32, (W, W), 0) == lax.broadcasted_iota(jnp.int32, (W, W), 1)
    a_row = [vec_ref[2:3, W * t : W * t + W] for t in range(4)]
    w_row = [vec_ref[3:4, W * t : W * t + W] for t in range(4)]

    def turn(row):
        return jnp.sum(jnp.where(eye, jnp.broadcast_to(row, (W, W)), 0.0), axis=1, keepdims=True)

    a_col = [turn(r) for r in a_row]
    w_col = [turn(r) for r in w_row]
    u_col = []
    v_row = []
    for t in range(4):
        at = PAIRS.index((t, 3)) * W
        u = gram_ref[at : at + W, :].astype(F32)[:, 116:117]
        u_col.append(u)
        u_row = jnp.sum(jnp.where(eye, jnp.broadcast_to(u, (W, W)), 0.0), axis=0, keepdims=True)
        v_row.append(u_row - count * a_row[t])
    for at, (i, j) in enumerate(PAIRS):
        s = gram_ref[W * at : W * at + W, :].astype(F32)
        x = (s - u_col[i] * a_row[j] - a_col[i] * v_row[j]) * (w_col[i] * inv_n) * w_row[j]
        if i == j:
            if i == 3:
                pad = (lax.broadcasted_iota(jnp.int32, (W, W), 0) >= 116).astype(F32)
                x = x + jnp.where(eye, pad + lam, 0.0)
            else:
                x = x + jnp.where(eye, lam, 0.0)
        m_ref[i, :, W * j : W * j + W] = x
    total = cross_ref[96 : 96 + TRAITS, 116:117]
    for t in range(4):
        c = cross_ref[32 * t : 32 * t + TRAITS, :]
        c_ref[:, W * t : W * t + W] = (c - total * a_row[t]) * (w_row[t] * inv_n)

    dot = functools.partial(lax.dot_general, precision=HI, preferred_element_type=F32)
    nn = (((1,), (0,)), ((), ()))
    tn = (((0,), (0,)), ((), ()))
    nt = (((1,), (1,)), ((), ()))
    d_ref[...] = m_ref[0, :, 0:W]

    def step(b, carry):
        tiles = invert([d_ref[8 * t : 8 * t + 8, :] for t in range(16)])
        for t in range(16):
            d_ref[8 * t : 8 * t + 8, :] = tiles[t]
        for s in range(4):
            @pl.when(b == s)
            def _():
                dinv = d_ref[...]
                lo = W * (s + 1)
                y = dot(c_ref[:, lo - W : lo], dinv, nn)
                c_ref[:, lo - W : lo] = y
                if s < 3:
                    right = m_ref[s, :, lo:]
                    t_new = dot(dinv, right, nn)
                    t_ref[s, :, lo:] = t_new
                    c_ref[:, lo:] = c_ref[:, lo:] - dot(y, right, nn)
                    for i in range(s + 1, 4):
                        left = m_ref[s, :, W * i : W * i + W]
                        m_ref[i, :, W * i :] = m_ref[i, :, W * i :] - dot(left, t_ref[s, :, W * i :], tn)
                    d_ref[...] = m_ref[s + 1, :, lo : lo + W]
        return carry

    lax.fori_loop(0, 4, step, 0)
    for s in (2, 1, 0):
        lo = W * (s + 1)
        c_ref[:, lo - W : lo] = c_ref[:, lo - W : lo] - dot(c_ref[:, lo:], t_ref[s, :, lo:], nt)
    out_ref[...] = c_ref[...].astype(jnp.bfloat16)


def solve(par, gram, cross, vec):
    return pl.pallas_call(
        solve_kernel,
        out_shape=jax.ShapeDtypeStruct((TRAITS, 512), jnp.bfloat16),
        in_specs=[pl.BlockSpec(memory_space=pltpu.SMEM)] + [pl.BlockSpec(memory_space=pltpu.VMEM)] * 3,
        out_specs=pl.BlockSpec(memory_space=pltpu.VMEM),
        scratch_shapes=[
            pltpu.VMEM((4, W, 512), F32),
            pltpu.VMEM((TRAITS, 512), F32),
            pltpu.VMEM((4, W, 512), F32),
            pltpu.VMEM((W, W), F32),
        ],
        compiler_params=pltpu.CompilerParams(vmem_limit_bytes=32 * 1024 * 1024),
    )(par, gram, cross, vec)


VMEM = pl.BlockSpec(memory_space=pltpu.VMEM)
SMEM = pl.BlockSpec(memory_space=pltpu.SMEM)
LIMIT = 48 * 1024 * 1024


def bounds():
    return [-(-(k * ROWS * 2 * CHIPS) // FOLDS) for k in range(FOLDS + 1)]


def first_fold(chip):
    return [k for k in range(FOLDS) if bounds()[k] <= chip * 2 * ROWS < bounds()[k + 1]][0]


STRADDLE = [c for c in range(CHIPS) if bounds()[first_fold(c) + 1] < (c + 1) * 2 * ROWS]


def gram_kernel(par_ref, order_ref, geno_ref, pheno_ref, vec_ref, part_ref, cross_ref, x_ref, g_ref, y_ref):
    bound = par_ref[0]
    lane = lax.broadcasted_iota(jnp.int32, (128, WIDE), 1)

    def chunk(i, carry):
        at = pl.multiple_of(i * 128, 128)
        for b in range(2):
            raw = geno_ref[pl.ds(at, 128), b * SNPS : (b + 1) * SNPS].astype(F32)
            raw = jnp.concatenate([raw, jnp.ones((128, WIDE - SNPS), F32)], axis=1)
            two_p = vec_ref[0:1, b * WIDE : (b + 1) * WIDE]
            spread = vec_ref[1:2, b * WIDE : (b + 1) * WIDE]
            x_ref[pl.ds(at, 128), b * WIDE : (b + 1) * WIDE] = ((raw - two_p) / spread).astype(BF16)
            g_ref[b, pl.ds(at, 128), :] = jnp.where(lane == SNPS, 1.0, raw - 1.0).astype(BF16)
        return carry

    lax.fori_loop(0, ROWS // 128, chunk, 0)
    rows = lax.broadcasted_iota(jnp.int32, (16, 32), 0)
    cols = lax.broadcasted_iota(jnp.int32, (16, 32), 1)
    pick = jnp.zeros((16, 32), F32)
    for q in range(TRAITS):
        pick = jnp.where((cols == q) & (rows == order_ref[q]), 1.0, pick)
    y_ref[...] = jnp.dot(pheno_ref[...], pick.astype(BF16), preferred_element_type=F32).astype(BF16)
    tn = (((0,), (0,)), ((), ()))
    row_ids = lax.broadcasted_iota(jnp.int32, (ROWS, 128), 0)
    for slot in range(2):
        def fill(slot=slot):
            keep = (row_ids < bound) if slot == 0 else (row_ids >= bound)
            y = jnp.where(keep[:, :32], y_ref[...], jnp.zeros((ROWS, 32), BF16))
            for b in range(2):
                at = 0
                for i in range(4):
                    left = g_ref[b, :, 128 * i : 128 * i + 128]
                    left = jnp.where(keep, left, jnp.zeros_like(left))
                    out = lax.dot_general(left, g_ref[b, :, 128 * i :], tn, preferred_element_type=F32)
                    out = out.astype(jnp.int32).astype(I16)
                    for j in range(4 - i):
                        part_ref[b, slot, at : at + 128, :] = out[:, 128 * j : 128 * j + 128]
                        at += 128
                out = lax.dot_general(y, g_ref[b], tn, preferred_element_type=F32)
                for t in range(4):
                    cross_ref[b, slot, 32 * t : 32 * t + 32, :] = out[:, 128 * t : 128 * t + 128]
        if slot == 0:
            fill()
        else:
            pl.when(bound < 2 * ROWS)(fill)


def grams(par, order, geno, pheno, vec):
    return pl.pallas_call(
        gram_kernel,
        out_shape=[
            jax.ShapeDtypeStruct((2, 2, CHIPS * SLICE, 128), I16),
            jax.ShapeDtypeStruct((2, 2, 128, 128), F32),
            jax.ShapeDtypeStruct((ROWS, 2 * WIDE), BF16),
        ],
        in_specs=[SMEM, SMEM, VMEM, VMEM, VMEM],
        out_specs=[VMEM, VMEM, VMEM],
        scratch_shapes=[pltpu.VMEM((2, ROWS, WIDE), BF16), pltpu.VMEM((ROWS, 32), BF16)],
        compiler_params=pltpu.CompilerParams(vmem_limit_bytes=LIMIT),
    )(par, order, geno, pheno, vec)


def remote(src, dst, send, recv, sample):
    return pltpu.make_async_remote_copy(
        src_ref=src, dst_ref=dst, send_sem=send, recv_sem=recv, device_id={"sample": sample}, device_id_type=MESH
    )


def reduce_kernel(
    part_ref, cross_ref, gram_ref, rhs_ref,
    sib, sib_x, mine, mine_x, got, got_x, got_b, got_xb, rest, rest_x,
    sib_sem, a_send, a_recv, b_send, b_recv, r_send, r_recv,
):
    me = lax.axis_index("sample")
    core = lax.rem(me, 2)
    chip = me // 2
    other = me + 1 - 2 * core
    straddles = (lax.rem(chip, 3) == 0) & (chip > 0) & (chip < 15)
    solver = (lax.rem(chip, 3) < 2) & (chip < 15)
    barrier = pltpu.get_barrier_semaphore()
    pl.semaphore_signal(barrier, inc=1, device_id={"sample": other}, device_id_type=MESH)
    for d in range(1, CHIPS):
        peer = 2 * lax.rem(chip + d, CHIPS) + core
        pl.semaphore_signal(barrier, inc=1, device_id={"sample": peer}, device_id_type=MESH)
    pl.semaphore_wait(barrier, CHIPS)

    def sibling(slot):
        return (
            remote(part_ref.at[1 - core, slot], sib.at[slot], sib_sem.at[0, slot], sib_sem.at[1, slot], other),
            remote(cross_ref.at[1 - core, slot], sib_x.at[slot], sib_sem.at[2, slot], sib_sem.at[3, slot], other),
        )

    def start_sibling(slot):
        for c in sibling(slot):
            c.start()

    def merge(slot):
        for c in sibling(slot):
            c.wait()

        def add(o, carry):
            at = pl.multiple_of(o * SLICE, 16)
            left = part_ref[core, slot, pl.ds(at, SLICE), :].astype(jnp.int32)
            right = sib[slot, pl.ds(at, SLICE), :].astype(jnp.int32)
            mine[slot, o] = (left + right).astype(I16)
            return carry

        lax.fori_loop(0, CHIPS, add, 0)
        for o in range(CHIPS):
            mine_x[slot, o] = cross_ref[core, slot, 8 * o : 8 * o + 8, :] + sib_x[slot, 8 * o : 8 * o + 8, :]

    def send_a(o, source):
        return (
            remote(mine.at[0, o], got.at[source], a_send.at[0, o], a_recv.at[0, source], 2 * o + core),
            remote(mine_x.at[0, o], got_x.at[source], a_send.at[1, o], a_recv.at[1, source], 2 * o + core),
        )

    def send_b(o, which):
        return (
            remote(mine.at[1, o], got_b.at[which], b_send.at[0, o], b_recv.at[0, which], 2 * o + core),
            remote(mine_x.at[1, o], got_xb.at[which], b_send.at[1, o], b_recv.at[1, which], 2 * o + core),
        )

    which = lax.max(chip // 3 - 1, 0)
    start_sibling(0)

    @pl.when(straddles)
    def _():
        start_sibling(1)

    merge(0)
    for d in range(1, CHIPS):
        for c in send_a(lax.rem(chip + d, CHIPS), chip):
            c.start()
    got[chip] = mine[0, chip]
    got_x[chip] = mine_x[0, chip]

    @pl.when(straddles)
    def _():
        merge(1)
        for d in range(1, CHIPS):
            for c in send_b(lax.rem(chip + d, CHIPS), which):
                c.start()
        got_b[which] = mine[1, chip]
        got_xb[which] = mine_x[1, chip]

    for d in range(1, CHIPS):
        source = lax.rem(chip + d, CHIPS)
        for c in send_a(source, source):
            c.wait()
    for w, source in enumerate(STRADDLE):
        @pl.when(chip != source)
        def _():
            for c in send_b(0, w):
                c.wait_recv()

    def sums(load_a, load_b):
        fold = []
        for k in range(FOLDS):
            parts = [load_a(c) for c in range(CHIPS) if first_fold(c) == k]
            parts += [load_b(w) for w, c in enumerate(STRADDLE) if first_fold(c) == k - 1]
            fold.append(functools.reduce(lambda p, q: p + q, parts))
        total = functools.reduce(lambda p, q: p + q, fold)
        return [total - f for f in fold]

    for i in range(SLICE // 16):
        rows = slice(16 * i, 16 * i + 16)
        values = sums(lambda c: got[c, rows, :].astype(jnp.int32), lambda w: got_b[w, rows, :].astype(jnp.int32))
        for k in range(FOLDS):
            rest[k, rows, :] = values[k].astype(I16)
    values = sums(lambda c: got_x[c], lambda w: got_xb[w])
    for k in range(FOLDS):
        rest_x[k] = values[k]

    def give(k, r, source):
        target = 2 * (3 * k + r) + core
        return (
            remote(rest.at[k], gram_ref.at[source], r_send.at[0, 2 * k + r], r_recv.at[0, source], target),
            remote(rest_x.at[k], rhs_ref.at[source], r_send.at[1, 2 * k + r], r_recv.at[1, source], target),
        )

    @pl.when(jnp.logical_not(solver))
    def _():
        gram_ref[...] = jnp.zeros_like(gram_ref)
        rhs_ref[...] = jnp.zeros_like(rhs_ref)

    for k in range(FOLDS):
        for r in range(2):
            @pl.when(chip != 3 * k + r)
            def _():
                for c in give(k, r, chip):
                    c.start()

            @pl.when(chip == 3 * k + r)
            def _():
                gram_ref[chip] = rest[k]
                rhs_ref[chip] = rest_x[k]

    @pl.when(straddles)
    def _():
        for d in range(1, CHIPS):
            for c in send_b(lax.rem(chip + d, CHIPS), which):
                c.wait_send()

    for k in range(FOLDS):
        for r in range(2):
            @pl.when(chip != 3 * k + r)
            def _():
                for c in give(k, r, chip):
                    c.wait_send()

    @pl.when(solver)
    def _():
        for d in range(1, CHIPS):
            for c in give(0, 0, lax.rem(chip + d, CHIPS)):
                c.wait_recv()


def reduce_grams(part, cross):
    dma = pltpu.SemaphoreType.DMA
    return pl.pallas_call(
        reduce_kernel,
        out_shape=[
            jax.ShapeDtypeStruct((CHIPS, SLICE, 128), I16),
            jax.ShapeDtypeStruct((CHIPS, 8, 128), F32),
        ],
        in_specs=[VMEM, VMEM],
        out_specs=[VMEM, VMEM],
        scratch_shapes=[
            pltpu.VMEM((2, CHIPS * SLICE, 128), I16),
            pltpu.VMEM((2, 128, 128), F32),
            pltpu.VMEM((2, CHIPS, SLICE, 128), I16),
            pltpu.VMEM((2, CHIPS, 8, 128), F32),
            pltpu.VMEM((CHIPS, SLICE, 128), I16),
            pltpu.VMEM((CHIPS, 8, 128), F32),
            pltpu.VMEM((4, SLICE, 128), I16),
            pltpu.VMEM((4, 8, 128), F32),
            pltpu.VMEM((FOLDS, SLICE, 128), I16),
            pltpu.VMEM((FOLDS, 8, 128), F32),
            dma((4, 2)),
            dma((2, CHIPS)),
            dma((2, CHIPS)),
            dma((2, CHIPS)),
            dma((2, 4)),
            dma((2, 2 * FOLDS)),
            dma((2, CHIPS)),
        ],
        compiler_params=pltpu.CompilerParams(collective_id=0, has_side_effects=True, vmem_limit_bytes=LIMIT),
    )(part, cross)


def predict_kernel(w_ref, x_ref, out_ref, got, stacked, send, w_send, w_recv, o_send, o_recv):
    me = lax.axis_index("sample")
    group = lax.axis_index("block")
    core = lax.rem(me, 2)
    chip = me // 2
    straddles = (lax.rem(chip, 3) == 0) & (chip > 0) & (chip < 15)
    solver = (lax.rem(chip, 3) < 2) & (chip < 15)
    barrier = pltpu.get_barrier_semaphore()
    pl.semaphore_signal(barrier, inc=1, device_id={"sample": me + 1 - 2 * core}, device_id_type=MESH)
    for d in (-3, -2, -1, 1, 2, 3):
        @pl.when((chip + d >= 0) & (chip + d < CHIPS))
        def _():
            for c in range(2):
                pl.semaphore_signal(barrier, inc=1, device_id={"sample": 2 * (chip + d) + c}, device_id_type=MESH)
    for d in range(1, 8):
        pl.semaphore_signal(barrier, inc=1, device_id={"block": lax.rem(group + d, 8)}, device_id_type=MESH)
    near = lax.min(chip, 3) + lax.min(CHIPS - 1 - chip, 3)
    pl.semaphore_wait(barrier, 8 + 2 * near)

    fold = chip // 3
    ridge = lax.rem(chip, 3)

    def give(m, c):
        slot = jnp.where(fold > 0, 1, 0) if m == 0 else 0
        place = 4 * slot + 2 * core + ridge
        return remote(w_ref, got.at[place], w_send.at[m, c], w_recv.at[place], 2 * (3 * fold + m) + c)

    @pl.when(solver)
    def _():
        for m in range(4):
            for c in range(2):
                mine = (ridge == m) & (core == c)

                @pl.when(jnp.logical_not(mine))
                def _():
                    give(m, c).start()

                @pl.when(mine)
                def _():
                    slot = jnp.where(fold > 0, 1, 0) if m == 0 else 0
                    got[4 * slot + 2 * core + ridge] = w_ref[...]

    first = jnp.where(chip > 0, (chip - 1) // 3, 0)

    def receive(slot, its_fold):
        for b in range(2):
            for r in range(2):
                @pl.when(jnp.logical_not((chip == 3 * its_fold + r) & (core == b)))
                def _():
                    place = 4 * slot + 2 * b + r
                    remote(w_ref, got.at[place], w_send.at[0, 0], w_recv.at[place], me + 1 - 2 * core).wait_recv()

    to = lax.broadcasted_iota(jnp.int32, (64, 64), 0)
    source = lax.broadcasted_iota(jnp.int32, (64, 64), 1)
    swap = (source == lax.rem(to, 4) * TRAITS + to // 4).astype(BF16)
    nt = (((1,), (1,)), ((), ()))

    def product(slot):
        stacked[...] = jnp.zeros_like(stacked)
        for b in range(2):
            for r in range(2):
                at = TRAITS * (2 * b + r)
                stacked[at : at + TRAITS, WIDE * b : WIDE * b + WIDE] = got[4 * slot + 2 * b + r]
        weights = jnp.dot(swap, stacked[...], preferred_element_type=F32).astype(BF16)
        return lax.dot_general(weights, x_ref[...], nt, preferred_element_type=F32)

    receive(0, first)
    out = product(0)
    for p in range(8):
        both = jnp.concatenate([out[8 * p : 8 * p + 8, :OUT_LANES], out[8 * p : 8 * p + 8, OUT_LANES:]], axis=0)
        send[p] = both.astype(BF16)

    @pl.when(straddles)
    def _():
        receive(1, fold)
        new = product(1)
        edge = jnp.int32(0)
        for k in range(1, FOLDS):
            edge = jnp.where(fold == k, bounds()[k], edge)
        half = lax.broadcasted_iota(jnp.int32, (16, OUT_LANES), 0) // 8
        sample = me * ROWS + half * OUT_LANES + lax.broadcasted_iota(jnp.int32, (16, OUT_LANES), 1)
        for p in range(8):
            both = jnp.concatenate([new[8 * p : 8 * p + 8, :OUT_LANES], new[8 * p : 8 * p + 8, OUT_LANES:]], axis=0)
            send[p] = jnp.where(sample >= edge, both, send[p].astype(F32)).astype(BF16)

    def exchange(p, source):
        return pltpu.make_async_remote_copy(
            src_ref=send.at[p], dst_ref=out_ref.at[source], send_sem=o_send.at[p], recv_sem=o_recv.at[source],
            device_id={"block": p}, device_id_type=MESH,
        )

    for d in range(1, 8):
        exchange(lax.rem(group + d, 8), group).start()
    out_ref[group] = send[group]

    @pl.when(solver)
    def _():
        for m in range(4):
            for c in range(2):
                @pl.when(jnp.logical_not((ridge == m) & (core == c)))
                def _():
                    give(m, c).wait_send()

    for d in range(1, 8):
        peer = lax.rem(group + d, 8)
        exchange(peer, peer).wait()


def predict(weights, x):
    dma = pltpu.SemaphoreType.DMA
    return pl.pallas_call(
        predict_kernel,
        out_shape=jax.ShapeDtypeStruct((8, 16, OUT_LANES), BF16),
        in_specs=[VMEM, VMEM],
        out_specs=VMEM,
        scratch_shapes=[
            pltpu.VMEM((8, TRAITS, WIDE), BF16),
            pltpu.VMEM((4 * TRAITS, 2 * WIDE), BF16),
            pltpu.VMEM((8, 16, OUT_LANES), BF16),
            dma((4, 2)),
            dma((8,)),
            dma((8,)),
            dma((8,)),
        ],
        compiler_params=pltpu.CompilerParams(collective_id=1, has_side_effects=True, vmem_limit_bytes=LIMIT),
    )(weights, x)


def shards(genotype, allele_freq, phenotype, shrinkage, owner_order):
    me = lax.axis_index("sample")
    chip = me // 2
    core = lax.rem(me, 2)
    freq = allele_freq.reshape(2, SNPS)
    spread = jnp.sqrt(2.0 * freq * (1.0 - freq))

    def pad(value, fill):
        return jnp.pad(value, ((0, 0), (0, WIDE - SNPS)), constant_values=fill).reshape(2 * WIDE)

    zero = jnp.zeros((2 * WIDE,), F32)
    vec = jnp.stack([pad(2.0 * freq, 1.0), pad(spread, 1.0), pad(2.0 * freq - 1.0, 0.0), pad(1.0 / spread, 0.0)] + [zero] * 4)
    edge = jnp.int32(3 * ROWS)
    count = jnp.float32(1.0)
    for c in STRADDLE:
        edge = jnp.where(chip == c, bounds()[first_fold(c) + 1] - me * ROWS, edge)
    for k in range(FOLDS):
        count = jnp.where(chip // 3 == k, float(2 * ROWS * CHIPS - bounds()[k + 1] + bounds()[k]), count)
    part, cross, x = grams(edge.reshape(1), owner_order, genotype, phenotype, vec)
    gram, rhs = reduce_grams(part, cross)
    lam = jnp.where(lax.rem(chip, 3) == 1, shrinkage[1], shrinkage[0])
    own = lax.dynamic_slice_in_dim(vec, core * WIDE, WIDE, 1)
    weights = solve(jnp.stack([lam, count]), gram.reshape(CHIPS * SLICE, 128), rhs.reshape(128, 128), own)
    got = predict(weights, x)
    return jnp.transpose(got.reshape(8, 2, 2, 4, OUT_LANES), (2, 0, 3, 1, 4)).reshape(2, 32, ROWS)


def solution(mesh):
    in_specs = (P("sample", "block"), P("block"), P("sample", None), P(), P())
    out_specs = P("block", None, "sample")
    return jax.shard_map(shards, mesh=mesh, in_specs=in_specs, out_specs=out_specs, check_vma=False)
```

time: 555 us -> 89.1 us (0.16); the launches traced: 544 us -> 88.9 us
  waiting for transfers between devices: 239 us -> 0 us
  other arithmetic: 157 us -> 0.78 us
  Pallas kernels: 0 us -> 79.3 us
  blocking collectives: 49.5 us -> 0 us
  local copies, waits for them, and re-layouts: 48.5 us -> 7.28 us
  matrix products: 31.1 us -> 0 us
  between operations: 18.6 us -> 1.51 us
    psum x1 -> x0, waiting for transfers between devices: 239 us -> none  [weights_for(): summed_grams, summed_crosses = lax.psum((grams, crosses), 'sample')]
    another operation x25 -> x1, other arithmetic: 128 us -> 0.08 us  [shards(): jnp.stack([lam, count])]
    pallas_call x0 -> x4, Pallas kernels: none -> 79.3 us  [the longest x1 34.5 us: reduce_grams(): pl.pallas_call(reduce_kernel, out_shape=[jax.ShapeDtypeStruct((CHIPS, SLI...]
    all_gather x1 -> x0, blocking collectives: 35.6 us -> none  [shared_solve(): collected = lax.all_gather(solved, 'sample', axis=0, tiled=True)]
    dot_general x48 -> x0, matrix products: 16.1 us -> none  [the longest x44 14.8 us: inner_products(): lax.dot_general(left_cols, right_cols, (((0,), (0,)), ((), ())), preferre...]
    another operation x20 -> x0, matrix products: 15 us -> none  [the longest x14 8.24 us: solve_pair(): return jax.scipy.linalg.cho_solve((factor, True), target)]
    all_to_all x1 -> x0, blocking collectives: 13.9 us -> none  [shards(): lax.all_to_all(local_preds, 'block', split_axis=0, concat_axis=1, tiled=T...]
    reduce_sum x2 -> x0, other arithmetic: 13.8 us -> none  [the longest x1 13.1 us: weights_for(): rest_grams = jnp.sum(whole, axis=0)[None] - whole]
  transfers between devices with their start and end apart: 1 -> 0, of which waited for: 1 -> 0; matrix products, arithmetic and copies ran while one was open for 0% -> 0% of each run, Pallas kernels for 0% -> 0%
where the time goes in v1:
time: 89.1 us; the launch traced here: 88.9 us
  Pallas kernels  79.3 us (89%)
  local copies, waits for them, and re-layouts  7.28 us (8%)
  between operations  1.51 us (2%)
    pallas_call x1, Pallas kernels, reduce_grams(): pl.pallas_call(reduce_kernel, out_shape=[jax.ShapeDtypeStruct((CHIPS, SLI...  34.5 us
    pallas_call x1, Pallas kernels, solve(): pl.pallas_call(solve_kernel, out_shape=jax.ShapeDtypeStruct((TRAITS, 512)...  20.5 us
    pallas_call x1, Pallas kernels, predict(): pl.pallas_call(predict_kernel, out_shape=jax.ShapeDtypeStruct((8, 16, OUT...  17.8 us
    pallas_call x1, Pallas kernels, grams(): pl.pallas_call(gram_kernel, out_shape=[jax.ShapeDtypeStruct((2, 2, CHIPS...  6.53 us
    unnamed x15, local copies, waits for them, and re-layouts  5.57 us

profile of v1, /device:TPU:34, one launch (start us, length us, event | category | flops | bytes accessed | tf_op | source)
XLA Modules:
  0.0 88.9 jit_solution(8009030591328858119)
XLA Ops:
  0.0 0.7 broadcast_subtract_fusion
  0.7 0.1 mul.22
  0.8 0.1 sub.39
  1.0 0.0 copy-start.1
  1.0 0.0 copy-start
  1.0 5.3 %copy.6.geno_ref = s32[1024,1000]{1,0:T(8,128)} copy(s32[1024,1000]{0,1:T(8,128)} %param.5) | data formatting | bytes 8192000 | tf_op args[0]
  6.4 0.0 copy-done.1
  6.4 0.0 copy-start.2
  6.4 0.2 copy.7.pheno_ref
  6.6 0.0 copy-done
  6.6 6.5 %shard_map.55 = (s16[2,2,1280,128]{3,2,1,0:T(8,128)(2,1)S(1)}, f32[2,2,128,128]{3,2,1,0:T(8,128)S(1)}, bf16[1024,1024]{1,0:T(8,128)(2,1)S(1)}) custom-call(s32[1]{0:T(128)} %bitcast.4.par_ref, s32[16]{0:T(128)S(1)} %copy-done, s32[1024,1000]{1,0:T(8,128)} %copy.6.geno_ref, bf16[1024,16]{1,0:T(8,128)(2,1)S(1)} %copy.7.pheno_ref, f32[8,1024]{1,0:T(8,128)S(1)} %stack.19.vec_ref), custom_call_target="tpu_custom_call" | custom-call | tf_op jit(solution)/shard_map/pallas_call | solution.py:217
  13.1 34.5 %shard_map.56 = (s16[16,80,128]{2,1,0:T(8,128)(2,1)S(1)}, f32[16,8,128]{2,1,0:T(8,128)S(1)}) custom-call(s16[2,2,1280,128]{3,2,1,0:T(8,128)(2,1)S(1)} %get-tuple-element.10.part_ref, f32[2,2,128,128]{3,2,1,0:T(8,128)S(1)} %get-tuple-element.11.cross_ref), custom_call_target="tpu_custom_call" | custom-call | tf_op jit(solution)/shard_map/pallas_call | solution.py:389
  47.7 0.0 copy-done.2
  47.7 0.6 fusion
  49.7 0.1 pad_maximum_fusion.par_ref
  49.7 20.5 %shard_map.57.w_ref = bf16[16,512]{1,0:T(8,128)(2,1)S(1)} custom-call(f32[2]{0:T(128)S(1)} %pad_maximum_fusion.par_ref, s16[1280,128]{1,0:T(8,128)(2,1)S(1)} %bitcast.24, f32[128,128]{1,0:T(8,128)S(1)} %bitcast.25, f32[8,512]{1,0:T(8,128)S(1)} %constant_dynamic-slice_fusion.vec_ref), custom_call_target="tpu_custom_call" | custom-call | tf_op jit(solution)/shard_map/pallas_call | solution.py:138
  70.3 17.8 %shard_map.58 = bf16[8,16,512]{2,1,0:T(8,128)(2,1)S(1)} custom-call(bf16[16,512]{1,0:T(8,128)(2,1)S(1)} %shard_map.57.w_ref, bf16[1024,1024]{1,0:T(8,128)(2,1)S(1)} %get-tuple-element.14.x_ref), custom_call_target="tpu_custom_call" | custom-call | tf_op jit(solution)/shard_map/pallas_call | solution.py:530
  88.1 0.1 copy.8
  88.2 0.7 reshape.24
  (12 shorter events, 0.2 us)
Async XLA Ops:
  1.0 5.4 %copy-start.1 = (bf16[1024,16]{0,1:T(8,128)(2,1)S(1)}, bf16[1024,16]{0,1:T(8,128)(2,1)}, u32[]{:S(2)}) copy-start(bf16[1024,16]{0,1:T(8,128)(2,1)} %param.7) | copy-start | bytes 98308
  1.0 5.5 %copy-start = (s32[16]{0:T(128)S(1)}, s32[16]{0:T(128)}, u32[]{:S(2)}) copy-start(s32[16]{0:T(128)} %order_ref.1) | copy-start | bytes 196
  6.4 41.3 %copy-start.2 = (f32[2]{0:T(128)S(1)}, f32[2]{0:T(128)}, u32[]{:S(2)}) copy-start(f32[2]{0:T(128)} %param.8) | copy-start | bytes 28

commit v2 on v1

v2 whole, which is shorter than its diff:
```python
import functools

import jax
import jax.numpy as jnp
from jax import lax
from jax.experimental import pallas as pl
from jax.experimental.pallas import tpu as pltpu
from jax.sharding import PartitionSpec as P

SNPS = 500
FOLDS = 5
WIDE = 512
ROWS = 1024
CHIPS = 16
SLICE = 64
OUT_LANES = 512
MESH = pl.DeviceIdType.MESH
BF16 = jnp.bfloat16
I16 = jnp.int16

W = 128
TRAITS = 16
PAIRS = [(i, j) for i in range(4) for j in range(i, 4)]
FULL = [(i, j) for i, j in PAIRS if i < j]
F32 = jnp.float32
HI = lax.Precision.HIGHEST


def row_of(x, i):
    return jnp.broadcast_to(x[i : i + 1, :], x.shape)


def lane_of(x, k):
    return jnp.broadcast_to(x[:, k : k + 1], x.shape)


def invert(tiles):
    sub = lax.broadcasted_iota(jnp.int32, (8, W), 0)
    lane = lax.broadcasted_iota(jnp.int32, (8, W), 1)
    for j in range(16):
        inside = (lane >= 8 * j) & (lane < 8 * j + 8)
        panel = tiles[j]
        cols = [lane_of(panel, 8 * j + i) for i in range(8)]
        rows = jnp.where(inside, (lane - 8 * j == sub).astype(F32), panel)
        for i in range(8):
            here = sub == i
            recip = 1.0 / row_of(cols[i], i)
            q = row_of(rows, i) * recip
            rows = jnp.where(here, q, rows - cols[i] * q)
            for c in range(i + 1, 8):
                qc = row_of(cols[c], i) * recip
                cols[c] = jnp.where(here, qc, cols[c] - cols[i] * qc)
        spread = [row_of(rows, i) for i in range(8)]
        new = []
        for t in range(16):
            if t == j:
                new.append(rows)
                continue
            acc = lane_of(tiles[t], 8 * j) * spread[0]
            for i in range(1, 8):
                acc = acc + lane_of(tiles[t], 8 * j + i) * spread[i]
            new.append(jnp.where(inside, 0.0, tiles[t]) - acc)
        tiles = new
    return tiles


def load_tile(ref, t):
    return jnp.concatenate([ref[2 * t], ref[2 * t + 1]], axis=0)


def load_rows(ref, t):
    return jnp.concatenate([ref[4 * t], ref[4 * t + 1]], axis=0)


def solve_part(lam, count, freq_row, gram_ref, cross_ref, out_ref, m_ref, c_ref, t_ref, d_ref):
    inv_n = 1.0 / count
    eye = lax.broadcasted_iota(jnp.int32, (W, W), 0) == lax.broadcasted_iota(jnp.int32, (W, W), 1)
    inside = lax.broadcasted_iota(jnp.int32, (1, WIDE), 1) < SNPS
    a_all = jnp.where(inside, 2.0 * freq_row - 1.0, 0.0)
    w_all = jnp.where(inside, 1.0 / jnp.sqrt(2.0 * freq_row * (1.0 - freq_row)), 0.0)
    a_row = [a_all[:, W * t : W * t + W] for t in range(4)]
    w_row = [w_all[:, W * t : W * t + W] for t in range(4)]

    def turn(row):
        return jnp.sum(jnp.where(eye, jnp.broadcast_to(row, (W, W)), 0.0), axis=1, keepdims=True)

    a_col = [turn(r) for r in a_row]
    w_col = [turn(r) for r in w_row]
    row = lax.broadcasted_iota(jnp.int32, (W, W), 0)
    lane = lax.broadcasted_iota(jnp.int32, (W, W), 1)

    def row_from(column):
        return jnp.sum(jnp.where(eye, jnp.broadcast_to(column, (W, W)), 0.0), axis=0, keepdims=True)

    sums = {p: load_tile(gram_ref, t).astype(F32) for t, p in enumerate(FULL)}
    for t in range(2):
        both = load_tile(gram_ref, 6 + t).astype(F32)
        turned = both.T
        low = pltpu.roll(both, W - 1, 0)
        if t == 0:
            low = jnp.where(row == W - 1, row_from(sums[0, 3][:, 117:118]), low)
        sums[2 * t, 2 * t] = jnp.where(row <= lane, both, turned)
        sums[2 * t + 1, 2 * t + 1] = jnp.where(row >= lane, low, low.T)
    u_col = [sums[t, 3][:, 116:117] for t in range(4)]
    v_row = [row_from(u_col[t]) - count * a_row[t] for t in range(4)]
    for i, j in PAIRS:
        s = sums[i, j]
        x = (s - u_col[i] * a_row[j] - a_col[i] * v_row[j]) * (w_col[i] * inv_n) * w_row[j]
        if i == j:
            if i == 3:
                pad = (lax.broadcasted_iota(jnp.int32, (W, W), 0) >= 116).astype(F32)
                x = x + jnp.where(eye, pad + lam, 0.0)
            else:
                x = x + jnp.where(eye, lam, 0.0)
        m_ref[i, :, W * j : W * j + W] = x
    total = load_rows(cross_ref, 3)[:, 116:117]
    for t in range(4):
        c = load_rows(cross_ref, t)
        c_ref[:, W * t : W * t + W] = (c - total * a_row[t]) * (w_row[t] * inv_n)

    dot = functools.partial(lax.dot_general, precision=HI, preferred_element_type=F32)
    nn = (((1,), (0,)), ((), ()))
    tn = (((0,), (0,)), ((), ()))
    nt = (((1,), (1,)), ((), ()))
    d_ref[...] = m_ref[0, :, 0:W]

    def step(b, carry):
        tiles = invert([d_ref[8 * t : 8 * t + 8, :] for t in range(16)])
        for t in range(16):
            d_ref[8 * t : 8 * t + 8, :] = tiles[t]
        for s in range(4):
            @pl.when(b == s)
            def _():
                dinv = d_ref[...]
                lo = W * (s + 1)
                y = dot(c_ref[:, lo - W : lo], dinv, nn)
                c_ref[:, lo - W : lo] = y
                if s < 3:
                    right = m_ref[s, :, lo:]
                    t_new = dot(dinv, right, nn)
                    t_ref[s, :, lo:] = t_new
                    c_ref[:, lo:] = c_ref[:, lo:] - dot(y, right, nn)
                    for i in range(s + 1, 4):
                        left = m_ref[s, :, W * i : W * i + W]
                        m_ref[i, :, W * i :] = m_ref[i, :, W * i :] - dot(left, t_ref[s, :, W * i :], tn)
                    d_ref[...] = m_ref[s + 1, :, lo : lo + W]
        return carry

    lax.fori_loop(0, 4, step, 0)
    for s in (2, 1, 0):
        lo = W * (s + 1)
        c_ref[:, lo - W : lo] = c_ref[:, lo - W : lo] - dot(c_ref[:, lo:], t_ref[s, :, lo:], nt)
    out_ref[...] = c_ref[...].astype(jnp.bfloat16)


VMEM = pl.BlockSpec(memory_space=pltpu.VMEM)
SMEM = pl.BlockSpec(memory_space=pltpu.SMEM)
LIMIT = 48 * 1024 * 1024


def bounds():
    return [-(-(k * ROWS * 2 * CHIPS) // FOLDS) for k in range(FOLDS + 1)]


def first_fold(chip):
    return [k for k in range(FOLDS) if bounds()[k] <= chip * 2 * ROWS < bounds()[k + 1]][0]


STRADDLE = [c for c in range(CHIPS) if bounds()[first_fold(c) + 1] < (c + 1) * 2 * ROWS]


def remote(src, dst, send, recv, sample):
    return pltpu.make_async_remote_copy(
        src_ref=src, dst_ref=dst, send_sem=send, recv_sem=recv, device_id={"sample": sample}, device_id_type=MESH
    )


def hop_from(chip, hop):
    return 8 * lax.rem(chip // 8 + hop[0], 2) + lax.rem(lax.rem(chip, 8) + hop[1] + 8, 8)


HOPS = [(x, z) for z in (4, 3, -3, 2, -2, 1, -1, 0) for x in (1, 0) if (x, z) != (0, 0)]


def reduce_part(
    barrier_wait, order_ref, geno_ref, pheno_ref, freq_ref, gram_ref, rhs_ref, x_ref,
    g_ref, y_ref, part, part_x,
    sib, sib_x, mine, mine_x, got, got_x, got_b, got_xb, rest, rest_x,
    sib_sem, a_send, a_recv, b_send, b_recv, r_send, r_recv,
):
    me = lax.axis_index("sample")
    core = lax.rem(me, 2)
    chip = me // 2
    other = me + 1 - 2 * core
    straddles = (lax.rem(chip, 3) == 0) & (chip > 0) & (chip < 15)
    solver = (lax.rem(chip, 3) < 2) & (chip < 15)

    def chip_at(hop):
        return hop_from(chip, hop)

    for b in range(2):
        for i in range(4):
            size = min(128, SNPS - 128 * i)
            at = b * SNPS + 128 * i
            g = (geno_ref[at : at + size, :] - 1).astype(F32)
            if size < 128:
                row = lax.broadcasted_iota(jnp.int32, (128 - size, ROWS), 0)
                g = jnp.concatenate([g, (row == 0).astype(F32)], axis=0)
            g_ref[b, 128 * i : 128 * i + 128, :] = g.astype(BF16)
    rows = lax.broadcasted_iota(jnp.int32, (32, TRAITS), 0)
    cols = lax.broadcasted_iota(jnp.int32, (32, TRAITS), 1)
    pick = jnp.zeros((32, TRAITS), F32)
    for q in range(TRAITS):
        pick = jnp.where((rows == q) & (cols == order_ref[q]), 1.0, pick)
    y_ref[...] = jnp.dot(pick.astype(BF16), pheno_ref[...], preferred_element_type=F32).astype(BF16)

    edge = jnp.int32(3 * ROWS)
    for c in STRADDLE:
        edge = jnp.where(chip == c, bounds()[first_fold(c) + 1], edge + 0)
    edge = jnp.where(straddles, edge - me * ROWS, 3 * ROWS)
    nt = (((1,), (1,)), ((), ()))
    eye = lax.broadcasted_iota(jnp.int32, (128, 128), 0) == lax.broadcasted_iota(jnp.int32, (128, 128), 1)
    up = lax.broadcasted_iota(jnp.int32, (128, 128), 0) <= lax.broadcasted_iota(jnp.int32, (128, 128), 1)
    lane = lax.broadcasted_iota(jnp.int32, (128, 128), 1)
    sample = lax.broadcasted_iota(jnp.int32, (128, ROWS), 1)

    def fill(b, slot):
        keep = (sample < edge) if slot == 0 else (sample >= edge)

        def times(left, right):
            left = jnp.where(keep[: left.shape[0]], left, jnp.zeros_like(left))
            return lax.dot_general(left, right, nt, preferred_element_type=F32)

        band = [times(g_ref[b, 128 * i : 128 * i + 128, :], g_ref[b, 128 * i :, :]) for i in range(4)]
        tile = {(i, j): band[i][:, 128 * (j - i) : 128 * (j - i) + 128] for i, j in PAIRS}
        tile[0, 3] = jnp.where(lane == 117, jnp.broadcast_to(tile[1, 1][:, 127:128], (128, 128)), tile[0, 3])
        packed = [tile[i, j] for i, j in FULL]
        packed += [jnp.where(up, tile[d, d], pltpu.roll(tile[d + 1, d + 1], 1, 0)) for d in (0, 2)]
        for t, value in enumerate(packed):
            part[b, slot, 128 * t : 128 * t + 128, :] = value.astype(jnp.int32).astype(I16)
        out = times(y_ref[...], g_ref[b])
        for t in range(4):
            part_x[b, slot, 32 * t : 32 * t + 32, :] = out[:, 128 * t : 128 * t + 128]

    def sibling(slot):
        return (
            remote(part.at[1 - core, slot], sib.at[slot], sib_sem.at[0, slot], sib_sem.at[1, slot], other),
            remote(part_x.at[1 - core, slot], sib_x.at[slot], sib_sem.at[2, slot], sib_sem.at[3, slot], other),
        )

    def start_sibling(slot):
        for c in sibling(slot):
            c.start()

    def merge(slot):
        for c in sibling(slot):
            c.wait()

        def add(o, carry):
            at = pl.multiple_of(o * SLICE, 16)
            left = part[core, slot, pl.ds(at, SLICE), :].astype(jnp.int32)
            right = sib[slot, pl.ds(at, SLICE), :].astype(jnp.int32)
            mine[slot, o] = (left + right).astype(I16)
            return carry

        lax.fori_loop(0, CHIPS, add, 0)
        for o in range(CHIPS):
            mine_x[slot, o] = part_x[core, slot, 8 * o : 8 * o + 8, :] + sib_x[slot, 8 * o : 8 * o + 8, :]

    def send_a(o, source):
        return (
            remote(mine.at[0, o], got.at[source], a_send.at[0, o], a_recv.at[0, source], 2 * o + core),
            remote(mine_x.at[0, o], got_x.at[source], a_send.at[1, o], a_recv.at[1, source], 2 * o + core),
        )

    def send_b(o, which):
        return (
            remote(mine.at[1, o], got_b.at[which], b_send.at[0, o], b_recv.at[0, which], 2 * o + core),
            remote(mine_x.at[1, o], got_xb.at[which], b_send.at[1, o], b_recv.at[1, which], 2 * o + core),
        )

    which = lax.max(chip // 3 - 1, 0)
    fill(1 - core, 0)
    barrier_wait()
    start_sibling(0)

    @pl.when(straddles)
    def _():
        fill(1 - core, 1)
        start_sibling(1)

    fill(core, 0)
    merge(0)
    for hop in HOPS:
        for c in send_a(chip_at(hop), chip):
            c.start()
    got[chip] = mine[0, chip]
    got_x[chip] = mine_x[0, chip]

    @pl.when(straddles)
    def _():
        fill(core, 1)
        merge(1)
        for hop in HOPS:
            for c in send_b(chip_at(hop), which):
                c.start()
        got_b[which] = mine[1, chip]
        got_xb[which] = mine_x[1, chip]

    for b in range(2):
        for i in range(4):
            size = min(128, SNPS - 128 * i)
            at = b * SNPS + 128 * i
            to = b * WIDE + 128 * i
            g = geno_ref[at : at + size, :]
            freq = jnp.broadcast_to(freq_ref[0:1, at : at + size], (size, size))
            freq = jnp.sum(jnp.where(eye[:size, :size], freq, 0.0), axis=1, keepdims=True)
            spread = jnp.sqrt(2.0 * freq * (1.0 - freq))
            zero, one, two = [(v - 2.0 * freq) / spread for v in (0.0, 1.0, 2.0)]
            x = jnp.where(g == 0, zero, jnp.where(g == 1, one, two))
            if size < 128:
                x = jnp.concatenate([x, jnp.zeros((128 - size, ROWS), F32)], axis=0)
            x_ref[to : to + 128, :] = x.astype(BF16)

    for hop in HOPS:
        source = chip_at(hop)
        for c in send_a(source, source):
            c.wait()
    for w, source in enumerate(STRADDLE):
        @pl.when(chip != source)
        def _():
            for c in send_b(0, w):
                c.wait_recv()

    def sums(load_a, load_b):
        fold = []
        for k in range(FOLDS):
            parts = [load_a(c) for c in range(CHIPS) if first_fold(c) == k]
            parts += [load_b(w) for w, c in enumerate(STRADDLE) if first_fold(c) == k - 1]
            fold.append(functools.reduce(lambda p, q: p + q, parts))
        total = functools.reduce(lambda p, q: p + q, fold)
        return [total - f for f in fold]

    for i in range(SLICE // 16):
        rows = slice(16 * i, 16 * i + 16)
        values = sums(lambda c: got[c, rows, :].astype(jnp.int32), lambda w: got_b[w, rows, :].astype(jnp.int32))
        for k in range(FOLDS):
            rest[k, rows, :] = values[k].astype(I16)
    values = sums(lambda c: got_x[c], lambda w: got_xb[w])
    for k in range(FOLDS):
        rest_x[k] = values[k]

    def give(k, r, source):
        target = 2 * (3 * k + r) + core
        return (
            remote(rest.at[k], gram_ref.at[source], r_send.at[0, 2 * k + r], r_recv.at[0, source], target),
            remote(rest_x.at[k], rhs_ref.at[source], r_send.at[1, 2 * k + r], r_recv.at[1, source], target),
        )

    for k in range(FOLDS):
        for r in range(2):
            @pl.when(chip != 3 * k + r)
            def _():
                for c in give(k, r, chip):
                    c.start()

            @pl.when(chip == 3 * k + r)
            def _():
                gram_ref[chip] = rest[k]
                rhs_ref[chip] = rest_x[k]

    @pl.when(straddles)
    def _():
        for hop in HOPS:
            for c in send_b(chip_at(hop), which):
                c.wait_send()

    for k in range(FOLDS):
        for r in range(2):
            @pl.when(chip != 3 * k + r)
            def _():
                for c in give(k, r, chip):
                    c.wait_send()

    @pl.when(solver)
    def _():
        for hop in HOPS:
            for c in give(0, 0, chip_at(hop)):
                c.wait_recv()


def predict_part(w_ref, x_ref, out_ref, got, stacked, send, w_send, w_recv, o_send, o_recv):
    me = lax.axis_index("sample")
    group = lax.axis_index("block")
    core = lax.rem(me, 2)
    chip = me // 2
    straddles = (lax.rem(chip, 3) == 0) & (chip > 0) & (chip < 15)
    solver = (lax.rem(chip, 3) < 2) & (chip < 15)
    fold = chip // 3
    ridge = lax.rem(chip, 3)

    def give(m, c):
        slot = jnp.where(fold > 0, 1, 0) if m == 0 else 0
        place = 4 * slot + 2 * core + ridge
        return remote(w_ref, got.at[place], w_send.at[m, c], w_recv.at[place], 2 * (3 * fold + m) + c)

    @pl.when(solver)
    def _():
        for m in range(4):
            for c in range(2):
                mine = (ridge == m) & (core == c)

                @pl.when(jnp.logical_not(mine))
                def _():
                    give(m, c).start()

                @pl.when(mine)
                def _():
                    slot = jnp.where(fold > 0, 1, 0) if m == 0 else 0
                    got[4 * slot + 2 * core + ridge] = w_ref[...]

    first = jnp.where(chip > 0, (chip - 1) // 3, 0)

    def receive(slot, its_fold):
        for b in range(2):
            for r in range(2):
                @pl.when(jnp.logical_not((chip == 3 * its_fold + r) & (core == b)))
                def _():
                    place = 4 * slot + 2 * b + r
                    remote(w_ref, got.at[place], w_send.at[0, 0], w_recv.at[place], me + 1 - 2 * core).wait_recv()

    to = lax.broadcasted_iota(jnp.int32, (64, 64), 0)
    source = lax.broadcasted_iota(jnp.int32, (64, 64), 1)
    swap = (source == lax.rem(to, 4) * TRAITS + to // 4).astype(BF16)

    def product(slots):
        stacked[...] = jnp.zeros_like(stacked)
        weights = []
        for slot in range(slots):
            for b in range(2):
                for r in range(2):
                    at = TRAITS * (2 * b + r)
                    stacked[at : at + TRAITS, WIDE * b : WIDE * b + WIDE] = got[4 * slot + 2 * b + r]
            weights.append(jnp.dot(swap, stacked[...], preferred_element_type=F32).astype(BF16))
        weights = jnp.concatenate(weights, axis=0)
        return jnp.dot(weights, x_ref[...], preferred_element_type=F32)

    def halves(out, p):
        return jnp.concatenate([out[8 * p : 8 * p + 8, :OUT_LANES], out[8 * p : 8 * p + 8, OUT_LANES:]], axis=0)

    receive(0, first)

    @pl.when(jnp.logical_not(straddles))
    def _():
        out = product(1)
        for p in range(8):
            send[p] = halves(out, p).astype(BF16)

    @pl.when(straddles)
    def _():
        receive(1, fold)
        out = product(2)
        edge = jnp.int32(0)
        for k in range(1, FOLDS):
            edge = jnp.where(fold == k, bounds()[k], edge)
        half = lax.broadcasted_iota(jnp.int32, (16, OUT_LANES), 0) // 8
        sample = me * ROWS + half * OUT_LANES + lax.broadcasted_iota(jnp.int32, (16, OUT_LANES), 1)
        for p in range(8):
            send[p] = jnp.where(sample >= edge, halves(out, p + 8), halves(out, p)).astype(BF16)

    def exchange(p, source):
        return pltpu.make_async_remote_copy(
            src_ref=send.at[p], dst_ref=out_ref.at[source], send_sem=o_send.at[p], recv_sem=o_recv.at[source],
            device_id={"block": p}, device_id_type=MESH,
        )

    for d in range(1, 8):
        exchange(lax.rem(group + d, 8), group).start()
    out_ref[group] = send[group]

    @pl.when(solver)
    def _():
        for m in range(4):
            for c in range(2):
                @pl.when(jnp.logical_not((ridge == m) & (core == c)))
                def _():
                    give(m, c).wait_send()

    for d in range(1, 8):
        peer = lax.rem(group + d, 8)
        exchange(peer, peer).wait()


def kernel(
    order_ref, shrink_ref, geno_ref, pheno_ref, freq_ref, out_ref,
    gram_ref, rhs_ref, x_ref, reduce_scratch, solve_scratch, w_ref, predict_scratch,
):
    me = lax.axis_index("sample")
    group = lax.axis_index("block")
    core = lax.rem(me, 2)
    chip = me // 2
    solver = (lax.rem(chip, 3) < 2) & (chip < 15)
    barrier = pltpu.get_barrier_semaphore()

    def greet(peer):
        pl.semaphore_signal(barrier, inc=1, device_id=peer, device_id_type=MESH)

    greet({"sample": me + 1 - 2 * core})
    for hop in HOPS:
        greet({"sample": 2 * hop_from(chip, hop) + core})
    for d in (-3, -2, -1, 1, 2, 3):
        @pl.when((chip + d >= 0) & (chip + d < CHIPS))
        def _():
            greet({"sample": 2 * (chip + d) + 1 - core})
    for d in range(1, 8):
        greet({"block": lax.rem(group + d, 8)})
    near = lax.min(chip, 3) + lax.min(CHIPS - 1 - chip, 3)

    def barrier_wait():
        pl.semaphore_wait(barrier, CHIPS + 7 + near)

    reduce_part(barrier_wait, order_ref, geno_ref, pheno_ref, freq_ref, gram_ref, rhs_ref, x_ref, *reduce_scratch)

    @pl.when(solver)
    def _():
        count = jnp.int32(1)
        for k in range(FOLDS):
            count = jnp.where(chip // 3 == k, 2 * ROWS * CHIPS - bounds()[k + 1] + bounds()[k], count)
        lam = jnp.where(lax.rem(chip, 3) == 1, shrink_ref[1], shrink_ref[0])
        freq = [
            jnp.concatenate([freq_ref[0:1, b * SNPS : (b + 1) * SNPS], jnp.full((1, WIDE - SNPS), 0.5, F32)], axis=1)
            for b in range(2)
        ]
        own = jnp.where(core == 0, freq[0], freq[1])
        solve_part(lam, count.astype(F32), own, gram_ref, rhs_ref, w_ref, *solve_scratch)

    predict_part(w_ref, x_ref, out_ref, *predict_scratch)


def call(order, shrinkage, geno, pheno, freq):
    dma = pltpu.SemaphoreType.DMA
    rows = CHIPS * SLICE
    return pl.pallas_call(
        kernel,
        out_shape=jax.ShapeDtypeStruct((8, 16, OUT_LANES), BF16),
        in_specs=[SMEM, SMEM, VMEM, VMEM, VMEM],
        out_specs=VMEM,
        scratch_shapes=[
            pltpu.VMEM((CHIPS, SLICE, 128), I16),
            pltpu.VMEM((CHIPS, 8, 128), F32),
            pltpu.VMEM((2 * WIDE, ROWS), BF16),
            [
                pltpu.VMEM((2, WIDE, ROWS), BF16),
                pltpu.VMEM((32, ROWS), BF16),
                pltpu.VMEM((2, 2, rows, 128), I16),
                pltpu.VMEM((2, 2, 128, 128), F32),
                pltpu.VMEM((2, rows, 128), I16),
                pltpu.VMEM((2, 128, 128), F32),
                pltpu.VMEM((2, CHIPS, SLICE, 128), I16),
                pltpu.VMEM((2, CHIPS, 8, 128), F32),
                pltpu.VMEM((CHIPS, SLICE, 128), I16),
                pltpu.VMEM((CHIPS, 8, 128), F32),
                pltpu.VMEM((4, SLICE, 128), I16),
                pltpu.VMEM((4, 8, 128), F32),
                pltpu.VMEM((FOLDS, SLICE, 128), I16),
                pltpu.VMEM((FOLDS, 8, 128), F32),
                dma((4, 2)),
                dma((2, CHIPS)),
                dma((2, CHIPS)),
                dma((2, CHIPS)),
                dma((2, 4)),
                dma((2, 2 * FOLDS)),
                dma((2, CHIPS)),
            ],
            [
                pltpu.VMEM((4, W, WIDE), F32),
                pltpu.VMEM((TRAITS, WIDE), F32),
                pltpu.VMEM((4, W, WIDE), F32),
                pltpu.VMEM((W, W), F32),
            ],
            pltpu.VMEM((TRAITS, WIDE), BF16),
            [
                pltpu.VMEM((8, TRAITS, WIDE), BF16),
                pltpu.VMEM((4 * TRAITS, 2 * WIDE), BF16),
                pltpu.VMEM((8, 16, OUT_LANES), BF16),
                dma((4, 2)),
                dma((8,)),
                dma((8,)),
                dma((8,)),
            ],
        ],
        compiler_params=pltpu.CompilerParams(collective_id=0, has_side_effects=True, vmem_limit_bytes=LIMIT),
    )(order, shrinkage, geno, pheno, freq)


def shards(genotype, allele_freq, phenotype, shrinkage, owner_order):
    got = call(owner_order, shrinkage, genotype.T, phenotype.T, allele_freq.reshape(1, 2 * SNPS))
    return jnp.transpose(got.reshape(8, 2, 2, 4, OUT_LANES), (2, 0, 3, 1, 4)).reshape(2, 32, ROWS)


def solution(mesh):
    in_specs = (P("sample", "block"), P("block"), P("sample", None), P(), P())
    out_specs = P("block", None, "sample")
    return jax.shard_map(shards, mesh=mesh, in_specs=in_specs, out_specs=out_specs, check_vma=False)
```

time: 89.1 us -> 70.9 us (0.80)
  Pallas kernels: 79.3 us -> 64.8 us
  local copies, waits for them, and re-layouts: 7.28 us -> 5.78 us
  between operations: 1.51 us -> 0.02 us
    pallas_call x4 -> x1, Pallas kernels: 79.3 us -> 64.8 us  [call(): pl.pallas_call(kernel, out_shape=jax.ShapeDtypeStruct((8, 16, OUT_LANES),...]
    unnamed x15 -> x10, local copies, waits for them, and re-layouts: 5.57 us -> 4.91 us
where the time goes in v2:
time: 70.9 us; the launch traced here: 70.6 us
  Pallas kernels  64.8 us (91%)
  local copies, waits for them, and re-layouts  5.78 us (8%)
    pallas_call x1, Pallas kernels, call(): pl.pallas_call(kernel, out_shape=jax.ShapeDtypeStruct((8, 16, OUT_LANES),...  64.8 us
    unnamed x10, local copies, waits for them, and re-layouts  4.91 us

profile of v2, /device:TPU:34, one launch (start us, length us, event | category | flops | bytes accessed | tf_op | source)
XLA Modules:
  0.0 70.6 jit_solution(9138754572828505516)
XLA Ops:
  0.0 0.0 copy-start
  0.0 2.2 %copy-done = s32[1024,1000]{0,1:T(8,128)S(1)} copy-done((s32[1024,1000]{0,1:T(8,128)S(1)}, s32[1024,1000]{0,1:T(8,128)}, u32[]{:S(2)}) %copy-start) | copy-done | bytes 4096024
  2.2 0.0 copy-start.1
  2.2 0.8 %copy-done.1 = bf16[1024,16]{0,1:T(8,128)(2,1)S(1)} copy-done((bf16[1024,16]{0,1:T(8,128)(2,1)S(1)}, bf16[1024,16]{0,1:T(8,128)(2,1)}, u32[]{:S(2)}) %copy-start.1) | copy-done | bytes 32792
  2.9 0.0 copy-start.2
  2.9 0.7 copy-done.2
  3.6 0.0 copy-start.3
  3.6 0.7 copy-done.3
  4.3 0.0 copy-start.4
  4.3 0.7 copy-done.4
  4.9 64.8 %shard_map.55 = bf16[8,16,512]{2,1,0:T(8,128)(2,1)S(1)} custom-call(s32[16]{0:T(128)S(1)} %copy-done.3, f32[2]{0:T(128)S(1)} %copy-done.4, s32[1000,1024]{1,0:T(8,128)S(1)} %bitcast.4, bf16[16,1024]{1,0:T(8,128)(2,1)S(1)} %bitcast.5, f32[1,1000]{1,0:T(1,128)S(1)} %bitcast.6), custom_call_target="tpu_custom_call" | custom-call | tf_op jit(solution)/shard_map/pallas_call | solution.py:543
  69.7 0.1 copy.6
  69.8 0.7 %reshape.11 = bf16[2,32,1024]{2,1,0:T(8,128)(2,1)} reshape(bf16[2,8,4,2,512]{4,3,2,1,0:T(2,128)(2,1)S(1)} %copy.6) | data formatting | bytes 262144 | tf_op jit(solution)/shard_map/reshape | solution.py:598
  (1 shorter events, 0.0 us)
Async XLA Ops:
  0.0 2.2 %copy-start = (s32[1024,1000]{0,1:T(8,128)S(1)}, s32[1024,1000]{0,1:T(8,128)}, u32[]{:S(2)}) copy-start(s32[1024,1000]{0,1:T(8,128)} %param.5) | copy-start | bytes 12288004
  2.2 0.8 %copy-start.1 = (bf16[1024,16]{0,1:T(8,128)(2,1)S(1)}, bf16[1024,16]{0,1:T(8,128)(2,1)}, u32[]{:S(2)}) copy-start(bf16[1024,16]{0,1:T(8,128)(2,1)} %param.7) | copy-start | bytes 98308
  2.9 0.7 copy-start.2
  3.6 0.7 copy-start.3
  4.3 0.7 copy-start.4

commit v3 on v2

--- a/solution.py
+++ b/solution.py
@@ -51,14 +51,19 @@
                 qc = row_of(cols[c], i) * recip
                 cols[c] = jnp.where(here, qc, cols[c] - cols[i] * qc)
         spread = [row_of(rows, i) for i in range(8)]
+        turned = jnp.where(lane < 8 * j, -panel, panel)
+        update = lax.dot_general(turned, rows, (((0,), (0,)), ((), ())), precision=HI, preferred_element_type=F32)
         new = []
         for t in range(16):
             if t == j:
                 new.append(rows)
                 continue
-            acc = lane_of(tiles[t], 8 * j) * spread[0]
-            for i in range(1, 8):
-                acc = acc + lane_of(tiles[t], 8 * j + i) * spread[i]
+            if t in (j + 1, j + 2):
+                acc = lane_of(tiles[t], 8 * j) * spread[0]
+                for i in range(1, 8):
+                    acc = acc + lane_of(tiles[t], 8 * j + i) * spread[i]
+            else:
+                acc = update[8 * t : 8 * t + 8, :]
             new.append(jnp.where(inside, 0.0, tiles[t]) - acc)
         tiles = new
     return tiles
@@ -69,7 +74,7 @@
 
 
 def load_rows(ref, t):
-    return jnp.concatenate([ref[4 * t], ref[4 * t + 1]], axis=0)
+    return ref[t]
 
 
 def solve_part(lam, count, freq_row, gram_ref, cross_ref, out_ref, m_ref, c_ref, t_ref, d_ref):
@@ -154,8 +159,9 @@
 
 
 VMEM = pl.BlockSpec(memory_space=pltpu.VMEM)
+HBM = pl.BlockSpec(memory_space=pltpu.HBM)
 SMEM = pl.BlockSpec(memory_space=pltpu.SMEM)
-LIMIT = 48 * 1024 * 1024
+LIMIT = 63 * 1024 * 1024
 
 
 def bounds():
@@ -166,6 +172,7 @@
     return [k for k in range(FOLDS) if bounds()[k] <= chip * 2 * ROWS < bounds()[k + 1]][0]
 
 
+CROSS_OWNERS = (2, 5, 11, 14)
 STRADDLE = [c for c in range(CHIPS) if bounds()[first_fold(c) + 1] < (c + 1) * 2 * ROWS]
 
 
@@ -183,10 +190,8 @@
 
 
 def reduce_part(
-    barrier_wait, order_ref, geno_ref, pheno_ref, freq_ref, gram_ref, rhs_ref, x_ref,
-    g_ref, y_ref, part, part_x,
-    sib, sib_x, mine, mine_x, got, got_x, got_b, got_xb, rest, rest_x,
-    sib_sem, a_send, a_recv, b_send, b_recv, r_send, r_recv,
+    load, settle_inputs, barrier_wait, order_ref, geno_ref, pheno_ref, freq_ref, gram_ref, rhs_ref, x_ref,
+    g_ref, y_ref, part, part_x, sib, sib_x, mine, mine_x, got, got_x, rest, rest_x, sib_sem, sems,
 ):
     me = lax.axis_index("sample")
     core = lax.rem(me, 2)
@@ -202,14 +207,16 @@
         for i in range(4):
             size = min(128, SNPS - 128 * i)
             at = b * SNPS + 128 * i
+            load(at + size)
             g = (geno_ref[at : at + size, :] - 1).astype(F32)
             if size < 128:
                 row = lax.broadcasted_iota(jnp.int32, (128 - size, ROWS), 0)
                 g = jnp.concatenate([g, (row == 0).astype(F32)], axis=0)
             g_ref[b, 128 * i : 128 * i + 128, :] = g.astype(BF16)
-    rows = lax.broadcasted_iota(jnp.int32, (32, TRAITS), 0)
-    cols = lax.broadcasted_iota(jnp.int32, (32, TRAITS), 1)
-    pick = jnp.zeros((32, TRAITS), F32)
+    settle_inputs()
+    rows = lax.broadcasted_iota(jnp.int32, (TRAITS, TRAITS), 0)
+    cols = lax.broadcasted_iota(jnp.int32, (TRAITS, TRAITS), 1)
+    pick = jnp.zeros((TRAITS, TRAITS), F32)
     for q in range(TRAITS):
         pick = jnp.where((rows == q) & (cols == order_ref[q]), 1.0, pick)
     y_ref[...] = jnp.dot(pick.astype(BF16), pheno_ref[...], preferred_element_type=F32).astype(BF16)
@@ -222,25 +229,37 @@
     eye = lax.broadcasted_iota(jnp.int32, (128, 128), 0) == lax.broadcasted_iota(jnp.int32, (128, 128), 1)
     up = lax.broadcasted_iota(jnp.int32, (128, 128), 0) <= lax.broadcasted_iota(jnp.int32, (128, 128), 1)
     lane = lax.broadcasted_iota(jnp.int32, (128, 128), 1)
-    sample = lax.broadcasted_iota(jnp.int32, (128, ROWS), 1)
-
-    def fill(b, slot):
-        keep = (sample < edge) if slot == 0 else (sample >= edge)
-
-        def times(left, right):
-            left = jnp.where(keep[: left.shape[0]], left, jnp.zeros_like(left))
-            return lax.dot_general(left, right, nt, preferred_element_type=F32)
-
-        band = [times(g_ref[b, 128 * i : 128 * i + 128, :], g_ref[b, 128 * i :, :]) for i in range(4)]
-        tile = {(i, j): band[i][:, 128 * (j - i) : 128 * (j - i) + 128] for i, j in PAIRS}
-        tile[0, 3] = jnp.where(lane == 117, jnp.broadcast_to(tile[1, 1][:, 127:128], (128, 128)), tile[0, 3])
-        packed = [tile[i, j] for i, j in FULL]
-        packed += [jnp.where(up, tile[d, d], pltpu.roll(tile[d + 1, d + 1], 1, 0)) for d in (0, 2)]
-        for t, value in enumerate(packed):
-            part[b, slot, 128 * t : 128 * t + 128, :] = value.astype(jnp.int32).astype(I16)
-        out = times(y_ref[...], g_ref[b])
-        for t in range(4):
-            part_x[b, slot, 32 * t : 32 * t + 32, :] = out[:, 128 * t : 128 * t + 128]
+    sample = lax.broadcasted_iota(jnp.int32, (1, ROWS), 1)
+
+    def fill(b, slots):
+        keeps = [sample < edge, sample >= edge][:slots]
+        if slots == 1:
+            keeps = [sample >= 0]
+        left = []
+        for keep in keeps:
+            for value in (g_ref[b], y_ref[...]):
+                left.append(value if slots == 1 else jnp.where(keep, value, jnp.zeros_like(value)))
+        height = WIDE + TRAITS
+        near = [left[2 * slot][0:256] if k == 0 else left[2 * slot + 1] for slot in range(slots) for k in range(2)]
+        band = [
+            lax.dot_general(jnp.concatenate(near, axis=0), g_ref[b, 0:256, :], nt, preferred_element_type=F32),
+            lax.dot_general(jnp.concatenate(left, axis=0), g_ref[b, 256:512, :], nt, preferred_element_type=F32),
+        ]
+        for slot in range(slots):
+            tops = [slot * (256 + TRAITS), slot * height]
+
+            def tile(i, j):
+                at = tops[j // 2] + 128 * i
+                return band[j // 2][at : at + 128, 128 * (j % 2) : 128 * (j % 2) + 128]
+
+            spare = jnp.broadcast_to(tile(1, 1)[:, 127:128], (128, 128))
+            packed = [jnp.where(lane == 117, spare, tile(i, j)) if (i, j) == (0, 3) else tile(i, j) for i, j in FULL]
+            packed += [jnp.where(up, tile(d, d), pltpu.roll(tile(d + 1, d + 1), 1, 0)) for d in (0, 2)]
+            for t, value in enumerate(packed):
+                part[b, slot, 128 * t : 128 * t + 128, :] = value.astype(jnp.int32).astype(I16)
+            for t in range(4):
+                at = tops[t // 2] + (256, WIDE)[t // 2]
+                part_x[b, slot, t] = band[t // 2][at : at + TRAITS, 128 * (t % 2) : 128 * (t % 2) + 128]
 
     def sibling(slot):
         return (
@@ -252,60 +271,60 @@
         for c in sibling(slot):
             c.start()
 
-    def merge(slot):
-        for c in sibling(slot):
-            c.wait()
-
-        def add(o, carry):
-            at = pl.multiple_of(o * SLICE, 16)
+    def add(o, slots):
+        at = pl.multiple_of(o * SLICE, 16)
+        for slot in range(slots):
             left = part[core, slot, pl.ds(at, SLICE), :].astype(jnp.int32)
             right = sib[slot, pl.ds(at, SLICE), :].astype(jnp.int32)
-            mine[slot, o] = (left + right).astype(I16)
-            return carry
-
-        lax.fori_loop(0, CHIPS, add, 0)
-        for o in range(CHIPS):
-            mine_x[slot, o] = part_x[core, slot, 8 * o : 8 * o + 8, :] + sib_x[slot, 8 * o : 8 * o + 8, :]
-
-    def send_a(o, source):
-        return (
-            remote(mine.at[0, o], got.at[source], a_send.at[0, o], a_recv.at[0, source], 2 * o + core),
-            remote(mine_x.at[0, o], got_x.at[source], a_send.at[1, o], a_recv.at[1, source], 2 * o + core),
-        )
-
-    def send_b(o, which):
-        return (
-            remote(mine.at[1, o], got_b.at[which], b_send.at[0, o], b_recv.at[0, which], 2 * o + core),
-            remote(mine_x.at[1, o], got_xb.at[which], b_send.at[1, o], b_recv.at[1, which], 2 * o + core),
-        )
-
-    which = lax.max(chip // 3 - 1, 0)
-    fill(1 - core, 0)
-    barrier_wait()
-    start_sibling(0)
+            mine[2 * o + slot] = (left + right).astype(I16)
+
+    def send_gram(slots):
+        for slot in range(slots):
+            for c in sibling(slot):
+                c.wait()
+        for hop in HOPS:
+            to = chip_at(hop)
+            add(to, slots)
+            here, there = pl.ds(2 * to, slots), pl.ds(2 * chip, slots)
+            remote(mine.at[here], got.at[there], sems.at[0], sems.at[1], 2 * to + core).start()
+        for t, owner in enumerate(CROSS_OWNERS):
+            for slot in range(slots):
+                mine_x[2 * t + slot] = part_x[core, slot, t] + sib_x[slot, t]
+
+            @pl.when(chip != owner)
+            def _():
+                here, there = pl.ds(2 * t, slots), pl.ds(2 * chip, slots)
+                remote(mine_x.at[here], got_x.at[there], sems.at[2], sems.at[3], 2 * owner + core).start()
+
+            @pl.when(chip == owner)
+            def _():
+                for slot in range(slots):
+                    got_x[2 * chip + slot] = mine_x[2 * t + slot]
+        add(chip, slots)
+        for slot in range(slots):
+            got[2 * chip + slot] = mine[2 * chip + slot]
+
+    def settle(array, count, sem, received):
+        c = remote(array.at[pl.ds(0, count)], array.at[pl.ds(0, count)], sems.at[sem], sems.at[sem], other)
+        c.wait_recv() if received else c.wait_send()
+
+    cross_owner = (lax.rem(chip, 3) == 2) & (chip != 8)
+
+    def local(slots):
+        fill(1 - core, slots)
+        barrier_wait()
+        for slot in range(slots):
+            start_sibling(slot)
+        fill(core, slots)
+        send_gram(slots)
+
+    @pl.when(jnp.logical_not(straddles))
+    def _():
+        local(1)
 
     @pl.when(straddles)
     def _():
-        fill(1 - core, 1)
-        start_sibling(1)
-
-    fill(core, 0)
-    merge(0)
-    for hop in HOPS:
-        for c in send_a(chip_at(hop), chip):
-            c.start()
-    got[chip] = mine[0, chip]
-    got_x[chip] = mine_x[0, chip]
-
-    @pl.when(straddles)
-    def _():
-        fill(core, 1)
-        merge(1)
-        for hop in HOPS:
-            for c in send_b(chip_at(hop), which):
-                c.start()
-        got_b[which] = mine[1, chip]
-        got_xb[which] = mine_x[1, chip]
+        local(2)
 
     for b in range(2):
         for i in range(4):
@@ -322,15 +341,13 @@
                 x = jnp.concatenate([x, jnp.zeros((128 - size, ROWS), F32)], axis=0)
             x_ref[to : to + 128, :] = x.astype(BF16)
 
-    for hop in HOPS:
-        source = chip_at(hop)
-        for c in send_a(source, source):
-            c.wait()
-    for w, source in enumerate(STRADDLE):
-        @pl.when(chip != source)
-        def _():
-            for c in send_b(0, w):
-                c.wait_recv()
+    @pl.when(straddles)
+    def _():
+        settle(got, 18, 1, True)
+
+    @pl.when(jnp.logical_not(straddles))
+    def _():
+        settle(got, 19, 1, True)
 
     def sums(load_a, load_b):
         fold = []
@@ -343,53 +360,72 @@
 
     for i in range(SLICE // 16):
         rows = slice(16 * i, 16 * i + 16)
-        values = sums(lambda c: got[c, rows, :].astype(jnp.int32), lambda w: got_b[w, rows, :].astype(jnp.int32))
+        values = sums(
+            lambda c: got[2 * c, rows, :].astype(jnp.int32), lambda w: got[2 * STRADDLE[w] + 1, rows, :].astype(jnp.int32)
+        )
         for k in range(FOLDS):
             rest[k, rows, :] = values[k].astype(I16)
-    values = sums(lambda c: got_x[c], lambda w: got_xb[w])
-    for k in range(FOLDS):
-        rest_x[k] = values[k]
-
-    def give(k, r, source):
-        target = 2 * (3 * k + r) + core
-        return (
-            remote(rest.at[k], gram_ref.at[source], r_send.at[0, 2 * k + r], r_recv.at[0, source], target),
-            remote(rest_x.at[k], rhs_ref.at[source], r_send.at[1, 2 * k + r], r_recv.at[1, source], target),
-        )
 
     for k in range(FOLDS):
         for r in range(2):
             @pl.when(chip != 3 * k + r)
             def _():
-                for c in give(k, r, chip):
-                    c.start()
+                remote(rest.at[k], gram_ref.at[chip], sems.at[4], sems.at[5], 2 * (3 * k + r) + core).start()
 
             @pl.when(chip == 3 * k + r)
             def _():
                 gram_ref[chip] = rest[k]
-                rhs_ref[chip] = rest_x[k]
+
+    @pl.when(cross_owner)
+    def _():
+        settle(got_x, 19, 3, True)
+        values = sums(lambda c: got_x[2 * c], lambda w: got_x[2 * STRADDLE[w] + 1])
+        for k in range(FOLDS):
+            rest_x[k] = values[k]
+        place = (chip - 2) // 3 - jnp.where(chip > 8, 1, 0)
+        for k in range(FOLDS):
+            for r in range(2):
+                remote(rest_x.at[k], rhs_ref.at[place], sems.at[6], sems.at[7], 2 * (3 * k + r) + core).start()
 
     @pl.when(straddles)
     def _():
-        for hop in HOPS:
-            for c in send_b(chip_at(hop), which):
-                c.wait_send()
-
-    for k in range(FOLDS):
-        for r in range(2):
-            @pl.when(chip != 3 * k + r)
-            def _():
-                for c in give(k, r, chip):
-                    c.wait_send()
+        settle(got, 30, 0, False)
+        settle(got_x, 8, 2, False)
+
+    @pl.when(jnp.logical_not(straddles))
+    def _():
+        settle(got, 15, 0, False)
+
+        @pl.when(cross_owner)
+        def _():
+            settle(got_x, 3, 2, False)
+
+        @pl.when(jnp.logical_not(cross_owner))
+        def _():
+            settle(got_x, 4, 2, False)
 
     @pl.when(solver)
     def _():
-        for hop in HOPS:
-            for c in give(0, 0, chip_at(hop)):
-                c.wait_recv()
-
-
-def predict_part(w_ref, x_ref, out_ref, got, stacked, send, w_send, w_recv, o_send, o_recv):
+        settle(got, 15, 5, True)
+        settle(got_x, 4, 7, True)
+
+    def finish():
+        @pl.when(solver)
+        def _():
+            settle(got, 9, 4, False)
+
+        @pl.when(jnp.logical_not(solver))
+        def _():
+            settle(got, 10, 4, False)
+
+        @pl.when(cross_owner)
+        def _():
+            settle(got_x, 10, 6, False)
+
+    finish()
+
+
+def predict_part(w_ref, x_ref, out_ref, got, stacked, send, landed, sems):
     me = lax.axis_index("sample")
     group = lax.axis_index("block")
     core = lax.rem(me, 2)
@@ -402,7 +438,7 @@
     def give(m, c):
         slot = jnp.where(fold > 0, 1, 0) if m == 0 else 0
         place = 4 * slot + 2 * core + ridge
-        return remote(w_ref, got.at[place], w_send.at[m, c], w_recv.at[place], 2 * (3 * fold + m) + c)
+        return remote(w_ref, got.at[place], sems.at[0], sems.at[1], 2 * (3 * fold + m) + c)
 
     @pl.when(solver)
     def _():
@@ -419,46 +455,41 @@
                     slot = jnp.where(fold > 0, 1, 0) if m == 0 else 0
                     got[4 * slot + 2 * core + ridge] = w_ref[...]
 
-    first = jnp.where(chip > 0, (chip - 1) // 3, 0)
-
-    def receive(slot, its_fold):
-        for b in range(2):
-            for r in range(2):
-                @pl.when(jnp.logical_not((chip == 3 * its_fold + r) & (core == b)))
-                def _():
-                    place = 4 * slot + 2 * b + r
-                    remote(w_ref, got.at[place], w_send.at[0, 0], w_recv.at[place], me + 1 - 2 * core).wait_recv()
-
-    to = lax.broadcasted_iota(jnp.int32, (64, 64), 0)
-    source = lax.broadcasted_iota(jnp.int32, (64, 64), 1)
-    swap = (source == lax.rem(to, 4) * TRAITS + to // 4).astype(BF16)
+    def settle(array, count, sem, received):
+        c = remote(array.at[pl.ds(0, count)], array.at[pl.ds(0, count)], sems.at[sem], sems.at[sem], me + 1 - 2 * core)
+        c.wait_recv() if received else c.wait_send()
 
     def product(slots):
-        stacked[...] = jnp.zeros_like(stacked)
-        weights = []
         for slot in range(slots):
             for b in range(2):
                 for r in range(2):
-                    at = TRAITS * (2 * b + r)
-                    stacked[at : at + TRAITS, WIDE * b : WIDE * b + WIDE] = got[4 * slot + 2 * b + r]
-            weights.append(jnp.dot(swap, stacked[...], preferred_element_type=F32).astype(BF16))
-        weights = jnp.concatenate(weights, axis=0)
+                    value = got[4 * slot + 2 * b + r].astype(F32)
+                    rows = pl.ds(64 * slot + 2 * b + r, TRAITS, stride=4)
+                    for t in range(4):
+                        stacked[4 * b + t, rows, :] = value[:, 128 * t : 128 * t + 128]
+        weights = jnp.concatenate([stacked[t, 0 : 64 * slots, :].astype(BF16) for t in range(8)], axis=1)
         return jnp.dot(weights, x_ref[...], preferred_element_type=F32)
 
     def halves(out, p):
         return jnp.concatenate([out[8 * p : 8 * p + 8, :OUT_LANES], out[8 * p : 8 * p + 8, OUT_LANES:]], axis=0)
 
-    receive(0, first)
-
     @pl.when(jnp.logical_not(straddles))
     def _():
+        @pl.when(solver)
+        def _():
+            settle(got, 3, 1, True)
+
+        @pl.when(jnp.logical_not(solver))
+        def _():
+            settle(got, 4, 1, True)
+
         out = product(1)
         for p in range(8):
             send[p] = halves(out, p).astype(BF16)
 
     @pl.when(straddles)
     def _():
-        receive(1, fold)
+        settle(got, 7, 1, True)
         out = product(2)
         edge = jnp.int32(0)
         for k in range(1, FOLDS):
@@ -468,33 +499,53 @@
         for p in range(8):
             send[p] = jnp.where(sample >= edge, halves(out, p + 8), halves(out, p)).astype(BF16)
 
-    def exchange(p, source):
-        return pltpu.make_async_remote_copy(
-            src_ref=send.at[p], dst_ref=out_ref.at[source], send_sem=o_send.at[p], recv_sem=o_recv.at[source],
-            device_id={"block": p}, device_id_type=MESH,
-        )
-
-    for d in range(1, 8):
-        exchange(lax.rem(group + d, 8), group).start()
-    out_ref[group] = send[group]
-
-    @pl.when(solver)
-    def _():
-        for m in range(4):
-            for c in range(2):
-                @pl.when(jnp.logical_not((ridge == m) & (core == c)))
-                def _():
-                    give(m, c).wait_send()
-
     for d in range(1, 8):
         peer = lax.rem(group + d, 8)
-        exchange(peer, peer).wait()
+        pltpu.make_async_remote_copy(
+            src_ref=send.at[peer], dst_ref=landed.at[group], send_sem=sems.at[2], recv_sem=sems.at[3],
+            device_id={"block": peer}, device_id_type=MESH,
+        ).start()
+    landed[group] = send[group]
+
+    @pl.when(solver)
+    def _():
+        settle(got, 7, 0, False)
+
+    settle(send, 7, 3, True)
+    low = lax.broadcasted_iota(jnp.int32, (8, OUT_LANES), 0) < 4
+    for half in range(2):
+        value = [landed[p].astype(F32)[8 * half : 8 * half + 8] for p in range(8)]
+        for q in range(2):
+            tiles = []
+            for p in range(0, 8, 2):
+                if q == 0:
+                    tiles.append(jnp.where(low, value[p], pltpu.roll(value[p + 1], 4, 0)))
+                else:
+                    tiles.append(jnp.where(low, pltpu.roll(value[p], 4, 0), value[p + 1]))
+            out_ref[q, :, OUT_LANES * half : OUT_LANES * (half + 1)] = jnp.concatenate(tiles, axis=0).astype(BF16)
+    settle(send, 7, 2, False)
 
 
 def kernel(
-    order_ref, shrink_ref, geno_ref, pheno_ref, freq_ref, out_ref,
+    order_ref, shrink_ref, geno_hbm, pheno_hbm, freq_hbm, out_ref, geno_ref, pheno_ref, freq_ref, in_sem,
     gram_ref, rhs_ref, x_ref, reduce_scratch, solve_scratch, w_ref, predict_scratch,
 ):
+    snps = geno_hbm.shape[0]
+    chunks = [slice(at, min(at + 128, snps)) for at in range(0, snps, 128)]
+    copies = [pltpu.make_async_copy(geno_hbm.at[c, :], geno_ref.at[c, :], in_sem.at[i]) for i, c in enumerate(chunks)]
+    copies += [
+        pltpu.make_async_copy(freq_hbm, freq_ref, in_sem.at[8]),
+        pltpu.make_async_copy(pheno_hbm, pheno_ref, in_sem.at[9]),
+    ]
+    for c in copies:
+        c.start()
+    loaded = [0]
+
+    def load(end):
+        while loaded[0] * 128 < end:
+            copies[loaded[0]].wait()
+            loaded[0] += 1
+
     me = lax.axis_index("sample")
     group = lax.axis_index("block")
     core = lax.rem(me, 2)
@@ -519,7 +570,12 @@
     def barrier_wait():
         pl.semaphore_wait(barrier, CHIPS + 7 + near)
 
-    reduce_part(barrier_wait, order_ref, geno_ref, pheno_ref, freq_ref, gram_ref, rhs_ref, x_ref, *reduce_scratch)
+    def settle_inputs():
+        copies[8].wait()
+        copies[9].wait()
+
+    predict_scratch[1][...] = jnp.zeros_like(predict_scratch[1])
+    reduce_part(load, settle_inputs, barrier_wait, order_ref, geno_ref, pheno_ref, freq_ref, gram_ref, rhs_ref, x_ref, *reduce_scratch)
 
     @pl.when(solver)
     def _():
@@ -542,35 +598,32 @@
     rows = CHIPS * SLICE
     return pl.pallas_call(
         kernel,
-        out_shape=jax.ShapeDtypeStruct((8, 16, OUT_LANES), BF16),
-        in_specs=[SMEM, SMEM, VMEM, VMEM, VMEM],
+        out_shape=jax.ShapeDtypeStruct((2, 32, ROWS), BF16),
+        in_specs=[SMEM, SMEM, HBM, HBM, HBM],
         out_specs=VMEM,
         scratch_shapes=[
+            pltpu.VMEM((2 * SNPS, ROWS), jnp.int32),
+            pltpu.VMEM((TRAITS, ROWS), BF16),
+            pltpu.VMEM((1, 2 * SNPS), F32),
+            dma((10,)),
             pltpu.VMEM((CHIPS, SLICE, 128), I16),
-            pltpu.VMEM((CHIPS, 8, 128), F32),
+            pltpu.VMEM((4, TRAITS, 128), F32),
             pltpu.VMEM((2 * WIDE, ROWS), BF16),
             [
                 pltpu.VMEM((2, WIDE, ROWS), BF16),
-                pltpu.VMEM((32, ROWS), BF16),
+                pltpu.VMEM((TRAITS, ROWS), BF16),
                 pltpu.VMEM((2, 2, rows, 128), I16),
-                pltpu.VMEM((2, 2, 128, 128), F32),
+                pltpu.VMEM((2, 2, 4, TRAITS, 128), F32),
                 pltpu.VMEM((2, rows, 128), I16),
-                pltpu.VMEM((2, 128, 128), F32),
-                pltpu.VMEM((2, CHIPS, SLICE, 128), I16),
-                pltpu.VMEM((2, CHIPS, 8, 128), F32),
-                pltpu.VMEM((CHIPS, SLICE, 128), I16),
-                pltpu.VMEM((CHIPS, 8, 128), F32),
-                pltpu.VMEM((4, SLICE, 128), I16),
-                pltpu.VMEM((4, 8, 128), F32),
+                pltpu.VMEM((2, 4, TRAITS, 128), F32),
+                pltpu.VMEM((2 * CHIPS, SLICE, 128), I16),
+                pltpu.VMEM((8, TRAITS, 128), F32),
+                pltpu.VMEM((2 * CHIPS, SLICE, 128), I16),
+                pltpu.VMEM((2 * CHIPS, TRAITS, 128), F32),
                 pltpu.VMEM((FOLDS, SLICE, 128), I16),
-                pltpu.VMEM((FOLDS, 8, 128), F32),
+                pltpu.VMEM((FOLDS, TRAITS, 128), F32),
                 dma((4, 2)),
-                dma((2, CHIPS)),
-                dma((2, CHIPS)),
-                dma((2, CHIPS)),
-                dma((2, 4)),
-                dma((2, 2 * FOLDS)),
-                dma((2, CHIPS)),
+                dma((8,)),
             ],
             [
                 pltpu.VMEM((4, W, WIDE), F32),
@@ -581,12 +634,10 @@
             pltpu.VMEM((TRAITS, WIDE), BF16),
             [
                 pltpu.VMEM((8, TRAITS, WIDE), BF16),
-                pltpu.VMEM((4 * TRAITS, 2 * WIDE), BF16),
+                pltpu.VMEM((8, 8 * TRAITS, 128), F32),
                 pltpu.VMEM((8, 16, OUT_LANES), BF16),
-                dma((4, 2)),
-                dma((8,)),
-                dma((8,)),
-                dma((8,)),
+                pltpu.VMEM((8, 16, OUT_LANES), BF16),
+                dma((4,)),
             ],
         ],
         compiler_params=pltpu.CompilerParams(collective_id=0, has_side_effects=True, vmem_limit_bytes=LIMIT),
@@ -594,8 +645,7 @@
 
 
 def shards(genotype, allele_freq, phenotype, shrinkage, owner_order):
-    got = call(owner_order, shrinkage, genotype.T, phenotype.T, allele_freq.reshape(1, 2 * SNPS))
-    return jnp.transpose(got.reshape(8, 2, 2, 4, OUT_LANES), (2, 0, 3, 1, 4)).reshape(2, 32, ROWS)
+    return call(owner_order, shrinkage, genotype.T, phenotype.T, allele_freq.reshape(1, 2 * SNPS))
 
 
 def solution(mesh):

time: 70.9 us -> 63.1 us (0.89)
  local copies, waits for them, and re-layouts: 5.78 us -> 1.57 us
  Pallas kernels: 64.8 us -> 61.4 us
    pallas_call x1, Pallas kernels: 64.8 us -> 61.4 us  [call(): pl.pallas_call(kernel, out_shape=jax.ShapeDtypeStruct((2, 32, ROWS), BF16...]
    unnamed x10 -> x1, local copies, waits for them, and re-layouts: 4.91 us -> 1.57 us
    reshape x2 -> x0, local copies, waits for them, and re-layouts: 0.76 us -> none  [the longest x1 0.73 us: shards(): jnp.transpose(got.reshape(8, 2, 2, 4, OUT_LANES), (2, 0, 3, 1, 4))]
where the time goes in v3:
time: 63.1 us; the launch traced here: 63 us
  Pallas kernels  61.4 us (97%)
  local copies, waits for them, and re-layouts  1.57 us (2%)
    pallas_call x1, Pallas kernels, call(): pl.pallas_call(kernel, out_shape=jax.ShapeDtypeStruct((2, 32, ROWS), BF16...  61.4 us
    unnamed x1, local copies, waits for them, and re-layouts  1.57 us

profile of v3, /device:TPU:34, one launch (start us, length us, event | category | flops | bytes accessed | tf_op | source)
XLA Modules:
  0.0 63.0 jit_solution(13591708114384719405)
XLA Ops:
  0.0 61.4 %shard_map.55 = bf16[2,32,1024]{2,1,0:T(8,128)(2,1)} custom-call(s32[16]{0:T(128)} %order_ref.1, f32[2]{0:T(128)} %shrink_ref.1, s32[1000,1024]{1,0:T(8,128)} %bitcast.3, bf16[16,1024]{1,0:T(8,128)(2,1)} %bitcast.4, f32[1,1000]{1,0:T(1,128)} %bitcast.5), custom_call_target="tpu_custom_call" | custom-call | tf_op jit(solution)/shard_map/pallas_call | solution.py:599
  61.4 1.6 %copy.7 = bf16[2,32,1024]{2,1,0:T(8,128)(2,1)} copy(bf16[2,32,1024]{2,1,0:T(8,128)(2,1)} %shard_map.55) | data formatting | bytes 262144

commit v4 on v3

--- a/solution.py
+++ b/solution.py
@@ -598,7 +598,7 @@
     rows = CHIPS * SLICE
     return pl.pallas_call(
         kernel,
-        out_shape=jax.ShapeDtypeStruct((2, 32, ROWS), BF16),
+        out_shape=pltpu.VMEM((2, 32, ROWS), BF16),
         in_specs=[SMEM, SMEM, HBM, HBM, HBM],
         out_specs=VMEM,
         scratch_shapes=[

time: 63.1 us -> 61.5 us (0.975)
  local copies, waits for them, and re-layouts: 1.57 us -> 0.66 us
  Pallas kernels: 61.4 us -> 60.7 us
    unnamed x1, local copies, waits for them, and re-layouts: 1.57 us -> 0.66 us
    pallas_call x1, Pallas kernels: 61.4 us -> 60.7 us  [call(): pl.pallas_call(kernel, out_shape=pltpu.VMEM((2, 32, ROWS), BF16), in_spec...]
where the time goes in v4:
time: 61.5 us; the launch traced here: 61.4 us
  Pallas kernels  60.7 us (99%)
  local copies, waits for them, and re-layouts  0.66 us (1%)
    pallas_call x1, Pallas kernels, call(): pl.pallas_call(kernel, out_shape=pltpu.VMEM((2, 32, ROWS), BF16), in_spec...  60.7 us

profile of v4, /device:TPU:34, one launch (start us, length us, event | category | flops | bytes accessed | tf_op | source)
XLA Modules:
  0.0 61.4 jit_solution(159233876703744594)
XLA Ops:
  0.0 60.7 %shard_map.55 = bf16[2,32,1024]{2,1,0:T(8,128)(2,1)S(1)} custom-call(s32[16]{0:T(128)} %order_ref.1, f32[2]{0:T(128)} %shrink_ref.1, s32[1000,1024]{1,0:T(8,128)} %bitcast.3, bf16[16,1024]{1,0:T(8,128)(2,1)} %bitcast.4, f32[1,1000]{1,0:T(1,128)} %bitcast.5), custom_call_target="tpu_custom_call" | custom-call | tf_op jit(solution)/shard_map/pallas_call | solution.py:599
  60.8 0.7 %copy.7 = bf16[2,32,1024]{2,1,0:T(8,128)(2,1)} copy(bf16[2,32,1024]{2,1,0:T(8,128)(2,1)S(1)} %shard_map.55) | data formatting | bytes 262144
